TPU v7x, 128 devices: a whole 4x4x4 slice. The times are simulated.
128 devices in a mesh: gx: 4 (over x), gy: 32 (over z, y, core).
Axes of the slice: x: 4, y: 4, z: 4, core: 2. Of those that a mesh axis runs over, the one named last changes fastest.
Arguments:
- particles: float32 [7, 1048576], P(None, ('gx', 'gy')), as said below
- pair_list: int32 [24576, 2], P(('gx', 'gy')), may hold values from 0 to 2047, as said below
- pair_count: int32 [128], P(('gx', 'gy')), may hold values from 144 to 192, as said below
Outputs:
- velocity: float32 [3, 1048576], P(None, ('gx', 'gy'))
- stretching: float32 [3, 1048576], P(None, ('gx', 'gy'))
Inputs may be any that keep to these rules, and one draw needn't show every extreme that they name: `particles`: row 6 (core radius) is positive; rows 0 to 5 are real-valued. `pair_list`: each listed pair, live or not, names two different clusters; with owners oa = A // 16 and ob = B // 16: oa <= ob <= oa + 6, and the pair stands in the slots of device (oa + ob) // 2. `pair_count`: some device is full in every draw.
All inputs are finite; a program needn't handle non-finite values.
Results may differ from a plain program's by a relative error of at most 0.0003.
Values sent between devices are 32-bit elements; how exact they have to be, the bound alone decides.
No kernel may reach another device: no remote copies, remote signals or barrier semaphores. Data moves between devices by JAX's collectives and lax.ppermute only.
A program may use at most 64 MiB of HBM per device.

v0:
```python
import jax
import jax.numpy as jnp
from jax import lax
from jax.sharding import PartitionSpec as P

CLUSTER = 512
REACH = 3


inv_four_pi = 0.07957747154594767


def passed_along(value, axis, steps):
    count = lax.axis_size(axis)
    first, last = (max(0, -steps), min(count, count - steps))
    return lax.ppermute(value, axis, [(source, source + steps) for source in range(first, last)])


def cross_list(left, right):
    return [
        left[1] * right[2] - left[2] * right[1],
        left[2] * right[0] - left[0] * right[2],
        left[0] * right[1] - left[1] * right[0],
    ]


def interact(first, second):
    radial = [first[c][:, None] - second[c][None, :] for c in range(3)]
    spread = 0.5 * (first[6][:, None] ** 2 + second[6][None, :] ** 2)
    rho = radial[0] * radial[0] + radial[1] * radial[1] + radial[2] * radial[2] + spread
    inverse = lax.rsqrt(rho)
    kernel = inverse * inverse * inverse
    steep = 3.0 * kernel * inverse * inverse
    alpha_first = [first[3 + c][:, None] for c in range(3)]
    alpha_second = [second[3 + c][None, :] for c in range(3)]
    cross_second = cross_list(radial, alpha_second)
    cross_first = cross_list(radial, alpha_first)
    proj_first = (
        alpha_first[0] * radial[0] + alpha_first[1] * radial[1] + alpha_first[2] * radial[2]
    )
    proj_second = (
        alpha_second[0] * radial[0] + alpha_second[1] * radial[1] + alpha_second[2] * radial[2]
    )
    vel_first = [-inv_four_pi * jnp.sum(kernel * cross_second[c], 1) for c in range(3)]
    vel_second = [inv_four_pi * jnp.sum(kernel * cross_first[c], 0) for c in range(3)]
    mixed_second = [jnp.sum(kernel * alpha_second[c], 1) for c in range(3)]
    mixed_first = [jnp.sum(kernel * alpha_first[c], 0) for c in range(3)]
    turn_first = cross_list([first[3 + c] for c in range(3)], mixed_second)
    turn_second = cross_list([second[3 + c] for c in range(3)], mixed_first)
    str_first = [
        -inv_four_pi * (turn_first[c] - jnp.sum(steep * proj_first * cross_second[c], 1))
        for c in range(3)
    ]
    str_second = [
        -inv_four_pi * (turn_second[c] - jnp.sum(steep * proj_second * cross_first[c], 0))
        for c in range(3)
    ]
    return (jnp.stack(vel_first + str_first), jnp.stack(vel_second + str_second))


def one_side(target, source):
    radial = [target[c][:, None] - source[c][None, :] for c in range(3)]
    spread = 0.5 * (target[6][:, None] ** 2 + source[6][None, :] ** 2)
    rho = radial[0] * radial[0] + radial[1] * radial[1] + radial[2] * radial[2] + spread
    inverse = lax.rsqrt(rho)
    kernel = inverse * inverse * inverse
    steep = 3.0 * kernel * inverse * inverse
    alpha_target = [target[3 + c][:, None] for c in range(3)]
    alpha_source = [source[3 + c][None, :] for c in range(3)]
    cross_source = cross_list(radial, alpha_source)
    proj_target = (
        alpha_target[0] * radial[0] + alpha_target[1] * radial[1] + alpha_target[2] * radial[2]
    )
    velocity_part = [-inv_four_pi * jnp.sum(kernel * cross_source[c], 1) for c in range(3)]
    mixed_source = [jnp.sum(kernel * alpha_source[c], 1) for c in range(3)]
    turn_target = cross_list([target[3 + c] for c in range(3)], mixed_source)
    stretch_part = [
        -inv_four_pi * (turn_target[c] - jnp.sum(steep * proj_target * cross_source[c], 1))
        for c in range(3)
    ]
    return jnp.stack(velocity_part + stretch_part)


def shards(particles, pair_list, pair_count):
    width = particles.shape[1]
    clusters_here = width // CLUSTER
    owned = particles.reshape(7, clusters_here, CLUSTER)
    owned_rows = jnp.moveaxis(owned, 1, 0)
    device = lax.axis_index(("gx", "gy"))
    own_terms = lax.map(lambda block: one_side(block, block), owned_rows)
    blocks = {0: owned}
    for offset in list(range(-REACH, 0)) + list(range(1, REACH + 1)):
        blocks[offset] = passed_along(owned, ("gx", "gy"), -offset)
    window = jnp.concatenate([blocks[offset] for offset in range(-REACH, REACH + 1)], axis=1)
    window_rows = jnp.moveaxis(window, 1, 0)
    window_size = window_rows.shape[0]
    anchor = (device - REACH) * clusters_here
    partial_value = jnp.zeros((window_size, 6, CLUSTER), jnp.float32)
    group = 8

    def visit(turn, carry):
        start = (turn * group).astype(jnp.int32)
        chosen = lax.dynamic_slice_in_dim(pair_list, start, group, 0)
        alive = start + jnp.arange(group, dtype=jnp.int32) < pair_count[0]
        first_id = jnp.clip(chosen[:, 0] - anchor, 0, window_size - 1)
        second_id = jnp.clip(chosen[:, 1] - anchor, 0, window_size - 1)
        upd_first, upd_second = jax.vmap(interact)(window_rows[first_id], window_rows[second_id])
        mask = alive[:, None, None]
        carry = carry.at[first_id].add(jnp.where(mask, upd_first, jnp.float32(0.0)))
        carry = carry.at[second_id].add(jnp.where(mask, upd_second, jnp.float32(0.0)))
        return carry

    turns = (pair_count[0] + group - 1) // group
    partial_value = lax.fori_loop(0, turns, visit, partial_value)
    pieces = partial_value.reshape(2 * REACH + 1, clusters_here, 6, CLUSTER)
    result = own_terms + pieces[REACH]
    for offset in list(range(-REACH, 0)) + list(range(1, REACH + 1)):
        result = result + passed_along(pieces[offset + REACH], ("gx", "gy"), offset)
    final = jnp.moveaxis(result, 0, 1).reshape(6, width)
    return (final[:3], final[3:])


def solution(mesh):
    placed = (P(None, ("gx", "gy")), P(("gx", "gy"), None), P(("gx", "gy")))
    return jax.shard_map(
        shards,
        mesh=mesh,
        in_specs=placed,
        out_specs=(P(None, ("gx", "gy")), P(None, ("gx", "gy"))),
        check_vma=False,
    )
```

profile of v0, /device:TPU:3, one launch (start us, length us, event | category | flops | bytes accessed | tf_op | source)
XLA Modules:
  0.0 1005.9 jit_solution(2121698062211940685)
XLA Ops:
  36.2 694.7 %while.21 = (s32[]{:T(128)}, f32[112,6,512]{2,1,0:T(8,128)S(1)}, s32[]{:T(128)}, s32[192,2]{0,1:T(2,128)S(1)}, s32[]{:T(128)}, /*index=5*/s32[1]{0:T(128)}, f32[...) while((s32[]{:T(128)}, f32[112,6,512]{2,1,0:T(8,128)S(1)}, s32[]{:T(128)}, ...), condition=%wide.region_32.33_spmd, body=%wide.region_11.32_spmd.sunk | while | flops 172148832 | bytes 4072059 | solution.py:114
  40.7 28.8 %fusion.108 = (f32[8,512]{1,0:T(8,128)S(1)}, f32[8,512]{1,0:T(8,128)S(1)}, f32[8,512]{1,0:T(8,128)S(1)}, f32[8,512]{1,0:T(8,128)S(1)}, f32[8,512]{1,0:T(8,128)S(...) fusion(f32[8,512]{1,0:T(8,128)S(1)} %bitcast.300, ...), kind=kLoop, calls=%fused_computation.115.clone.1 | loop fusion | flops 171892736 | bytes 524288 | tf_op jit(solution)/shard_map/while/body/vmap()/reduce_sum | solution.py:55
  77.3 28.8 %fusion.108 = (f32[8,512]{1,0:T(8,128)S(1)}, f32[8,512]{1,0:T(8,128)S(1)}, f32[8,512]{1,0:T(8,128)S(1)}, f32[8,512]{1,0:T(8,128)S(1)}, f32[8,512]{1,0:T(8,128)S(...) fusion(f32[8,512]{1,0:T(8,128)S(1)} %bitcast.300, ...), kind=kLoop, calls=%fused_computation.115.clone.1 | loop fusion | flops 171892736 | bytes 524288 | tf_op jit(solution)/shard_map/while/body/vmap()/reduce_sum | solution.py:55
  113.9 28.8 %fusion.108 = (f32[8,512]{1,0:T(8,128)S(1)}, f32[8,512]{1,0:T(8,128)S(1)}, f32[8,512]{1,0:T(8,128)S(1)}, f32[8,512]{1,0:T(8,128)S(1)}, f32[8,512]{1,0:T(8,128)S(...) fusion(f32[8,512]{1,0:T(8,128)S(1)} %bitcast.300, ...), kind=kLoop, calls=%fused_computation.115.clone.1 | loop fusion | flops 171892736 | bytes 524288 | tf_op jit(solution)/shard_map/while/body/vmap()/reduce_sum | solution.py:55
  150.4 28.8 %fusion.108 = (f32[8,512]{1,0:T(8,128)S(1)}, f32[8,512]{1,0:T(8,128)S(1)}, f32[8,512]{1,0:T(8,128)S(1)}, f32[8,512]{1,0:T(8,128)S(1)}, f32[8,512]{1,0:T(8,128)S(...) fusion(f32[8,512]{1,0:T(8,128)S(1)} %bitcast.300, ...), kind=kLoop, calls=%fused_computation.115.clone.1 | loop fusion | flops 171892736 | bytes 524288 | tf_op jit(solution)/shard_map/while/body/vmap()/reduce_sum | solution.py:55
  187.0 28.8 %fusion.108 = (f32[8,512]{1,0:T(8,128)S(1)}, f32[8,512]{1,0:T(8,128)S(1)}, f32[8,512]{1,0:T(8,128)S(1)}, f32[8,512]{1,0:T(8,128)S(1)}, f32[8,512]{1,0:T(8,128)S(...) fusion(f32[8,512]{1,0:T(8,128)S(1)} %bitcast.300, ...), kind=kLoop, calls=%fused_computation.115.clone.1 | loop fusion | flops 171892736 | bytes 524288 | tf_op jit(solution)/shard_map/while/body/vmap()/reduce_sum | solution.py:55
  223.6 28.8 %fusion.108 = (f32[8,512]{1,0:T(8,128)S(1)}, f32[8,512]{1,0:T(8,128)S(1)}, f32[8,512]{1,0:T(8,128)S(1)}, f32[8,512]{1,0:T(8,128)S(1)}, f32[8,512]{1,0:T(8,128)S(...) fusion(f32[8,512]{1,0:T(8,128)S(1)} %bitcast.300, ...), kind=kLoop, calls=%fused_computation.115.clone.1 | loop fusion | flops 171892736 | bytes 524288 | tf_op jit(solution)/shard_map/while/body/vmap()/reduce_sum | solution.py:55
  260.1 28.8 %fusion.108 = (f32[8,512]{1,0:T(8,128)S(1)}, f32[8,512]{1,0:T(8,128)S(1)}, f32[8,512]{1,0:T(8,128)S(1)}, f32[8,512]{1,0:T(8,128)S(1)}, f32[8,512]{1,0:T(8,128)S(...) fusion(f32[8,512]{1,0:T(8,128)S(1)} %bitcast.300, ...), kind=kLoop, calls=%fused_computation.115.clone.1 | loop fusion | flops 171892736 | bytes 524288 | tf_op jit(solution)/shard_map/while/body/vmap()/reduce_sum | solution.py:55
  296.7 28.8 %fusion.108 = (f32[8,512]{1,0:T(8,128)S(1)}, f32[8,512]{1,0:T(8,128)S(1)}, f32[8,512]{1,0:T(8,128)S(1)}, f32[8,512]{1,0:T(8,128)S(1)}, f32[8,512]{1,0:T(8,128)S(...) fusion(f32[8,512]{1,0:T(8,128)S(1)} %bitcast.300, ...), kind=kLoop, calls=%fused_computation.115.clone.1 | loop fusion | flops 171892736 | bytes 524288 | tf_op jit(solution)/shard_map/while/body/vmap()/reduce_sum | solution.py:55
  333.3 28.8 %fusion.108 = (f32[8,512]{1,0:T(8,128)S(1)}, f32[8,512]{1,0:T(8,128)S(1)}, f32[8,512]{1,0:T(8,128)S(1)}, f32[8,512]{1,0:T(8,128)S(1)}, f32[8,512]{1,0:T(8,128)S(...) fusion(f32[8,512]{1,0:T(8,128)S(1)} %bitcast.300, ...), kind=kLoop, calls=%fused_computation.115.clone.1 | loop fusion | flops 171892736 | bytes 524288 | tf_op jit(solution)/shard_map/while/body/vmap()/reduce_sum | solution.py:55
  369.8 28.8 %fusion.108 = (f32[8,512]{1,0:T(8,128)S(1)}, f32[8,512]{1,0:T(8,128)S(1)}, f32[8,512]{1,0:T(8,128)S(1)}, f32[8,512]{1,0:T(8,128)S(1)}, f32[8,512]{1,0:T(8,128)S(...) fusion(f32[8,512]{1,0:T(8,128)S(1)} %bitcast.300, ...), kind=kLoop, calls=%fused_computation.115.clone.1 | loop fusion | flops 171892736 | bytes 524288 | tf_op jit(solution)/shard_map/while/body/vmap()/reduce_sum | solution.py:55
  406.4 28.8 %fusion.108 = (f32[8,512]{1,0:T(8,128)S(1)}, f32[8,512]{1,0:T(8,128)S(1)}, f32[8,512]{1,0:T(8,128)S(1)}, f32[8,512]{1,0:T(8,128)S(1)}, f32[8,512]{1,0:T(8,128)S(...) fusion(f32[8,512]{1,0:T(8,128)S(1)} %bitcast.300, ...), kind=kLoop, calls=%fused_computation.115.clone.1 | loop fusion | flops 171892736 | bytes 524288 | tf_op jit(solution)/shard_map/while/body/vmap()/reduce_sum | solution.py:55
  443.0 28.8 %fusion.108 = (f32[8,512]{1,0:T(8,128)S(1)}, f32[8,512]{1,0:T(8,128)S(1)}, f32[8,512]{1,0:T(8,128)S(1)}, f32[8,512]{1,0:T(8,128)S(1)}, f32[8,512]{1,0:T(8,128)S(...) fusion(f32[8,512]{1,0:T(8,128)S(1)} %bitcast.300, ...), kind=kLoop, calls=%fused_computation.115.clone.1 | loop fusion | flops 171892736 | bytes 524288 | tf_op jit(solution)/shard_map/while/body/vmap()/reduce_sum | solution.py:55
  479.5 28.8 %fusion.108 = (f32[8,512]{1,0:T(8,128)S(1)}, f32[8,512]{1,0:T(8,128)S(1)}, f32[8,512]{1,0:T(8,128)S(1)}, f32[8,512]{1,0:T(8,128)S(1)}, f32[8,512]{1,0:T(8,128)S(...) fusion(f32[8,512]{1,0:T(8,128)S(1)} %bitcast.300, ...), kind=kLoop, calls=%fused_computation.115.clone.1 | loop fusion | flops 171892736 | bytes 524288 | tf_op jit(solution)/shard_map/while/body/vmap()/reduce_sum | solution.py:55
  516.1 28.8 %fusion.108 = (f32[8,512]{1,0:T(8,128)S(1)}, f32[8,512]{1,0:T(8,128)S(1)}, f32[8,512]{1,0:T(8,128)S(1)}, f32[8,512]{1,0:T(8,128)S(1)}, f32[8,512]{1,0:T(8,128)S(...) fusion(f32[8,512]{1,0:T(8,128)S(1)} %bitcast.300, ...), kind=kLoop, calls=%fused_computation.115.clone.1 | loop fusion | flops 171892736 | bytes 524288 | tf_op jit(solution)/shard_map/while/body/vmap()/reduce_sum | solution.py:55
  552.7 28.8 %fusion.108 = (f32[8,512]{1,0:T(8,128)S(1)}, f32[8,512]{1,0:T(8,128)S(1)}, f32[8,512]{1,0:T(8,128)S(1)}, f32[8,512]{1,0:T(8,128)S(1)}, f32[8,512]{1,0:T(8,128)S(...) fusion(f32[8,512]{1,0:T(8,128)S(1)} %bitcast.300, ...), kind=kLoop, calls=%fused_computation.115.clone.1 | loop fusion | flops 171892736 | bytes 524288 | tf_op jit(solution)/shard_map/while/body/vmap()/reduce_sum | solution.py:55
  589.2 28.8 %fusion.108 = (f32[8,512]{1,0:T(8,128)S(1)}, f32[8,512]{1,0:T(8,128)S(1)}, f32[8,512]{1,0:T(8,128)S(1)}, f32[8,512]{1,0:T(8,128)S(1)}, f32[8,512]{1,0:T(8,128)S(...) fusion(f32[8,512]{1,0:T(8,128)S(1)} %bitcast.300, ...), kind=kLoop, calls=%fused_computation.115.clone.1 | loop fusion | flops 171892736 | bytes 524288 | tf_op jit(solution)/shard_map/while/body/vmap()/reduce_sum | solution.py:55
  625.8 28.8 %fusion.108 = (f32[8,512]{1,0:T(8,128)S(1)}, f32[8,512]{1,0:T(8,128)S(1)}, f32[8,512]{1,0:T(8,128)S(1)}, f32[8,512]{1,0:T(8,128)S(1)}, f32[8,512]{1,0:T(8,128)S(...) fusion(f32[8,512]{1,0:T(8,128)S(1)} %bitcast.300, ...), kind=kLoop, calls=%fused_computation.115.clone.1 | loop fusion | flops 171892736 | bytes 524288 | tf_op jit(solution)/shard_map/while/body/vmap()/reduce_sum | solution.py:55
  698.9 28.8 %fusion.108 = (f32[8,512]{1,0:T(8,128)S(1)}, f32[8,512]{1,0:T(8,128)S(1)}, f32[8,512]{1,0:T(8,128)S(1)}, f32[8,512]{1,0:T(8,128)S(1)}, f32[8,512]{1,0:T(8,128)S(...) fusion(f32[8,512]{1,0:T(8,128)S(1)} %bitcast.300, ...), kind=kLoop, calls=%fused_computation.115.clone.1 | loop fusion | flops 171892736 | bytes 524288 | tf_op jit(solution)/shard_map/while/body/vmap()/reduce_sum | solution.py:55
  731.8 36.1 %collective-permute-start.10 = (f32[16,6,512]{2,1,0:T(8,128)}, f32[16,6,512]{2,1,0:T(8,128)S(1)}, u32[]{:S(2)}, u32[]{:S(2)}) collective-permute-start(f32[16,6,512]{2,1,0:T(8,128)} %get-tuple-element.146), channel_id=1, source_target_pairs={{0,2},{1,3},{2,4},{3,5},{4,6},{5,7},{6,8},{7,9},{8,10},{9,11},{10,... | collective-permute-start | bytes 589832 | tf_op jit(solution)/shard_map/ppermute | solution.py:16
  767.9 80.0 %collective-permute-start.11 = (f32[16,6,512]{2,1,0:T(8,128)}, f32[16,6,512]{2,1,0:T(8,128)S(1)}, u32[]{:S(2)}, u32[]{:S(2)}) collective-permute-start(f32[16,6,512]{2,1,0:T(8,128)} %get-tuple-element.145), channel_id=1, source_target_pairs={{0,3},{1,4},{2,5},{3,6},{4,7},{5,8},{6,9},{7,10},{8,11},{9,12},{10... | collective-permute-start | bytes 589832 | tf_op jit(solution)/shard_map/ppermute | solution.py:16
  854.5 31.1 %collective-permute-start.7 = (f32[16,6,512]{2,1,0:T(8,128)S(1)}, f32[16,6,512]{2,1,0:T(8,128)}, u32[]{:S(2)}, u32[]{:S(2)}) collective-permute-start(f32[16,6,512]{2,1,0:T(8,128)S(1)} %get-tuple-element.149), channel_id=1, source_target_pairs={{2,0},{3,1},{4,2},{5,3},{6,4},{7,5},{8,6},{9,7},{10,8},{11,9},{12,... | collective-permute-start | bytes 589832 | tf_op jit(solution)/shard_map/ppermute | solution.py:16
  885.5 48.7 %collective-permute-start.8 = (f32[16,6,512]{2,1,0:T(8,128)S(1)}, f32[16,6,512]{2,1,0:T(8,128)}, u32[]{:S(2)}, u32[]{:S(2)}) collective-permute-start(f32[16,6,512]{2,1,0:T(8,128)S(1)} %get-tuple-element.148), channel_id=1, source_target_pairs={{1,0},{2,1},{3,2},{4,3},{5,4},{6,5},{7,6},{8,7},{9,8},{10,9},{11,1... | collective-permute-start | bytes 589832 | tf_op jit(solution)/shard_map/ppermute | solution.py:16
  936.2 67.5 %while.20 = (s32[]{:T(128)}, f32[16,6,512]{2,1,0:T(8,128)}, f32[16,7,512]{2,1,0:T(8,128)}, s32[]{:T(128)}, s32[]{:T(128)}, /*index=5*/s32[]{}, s32[]{}, s32[]{}, s32[]{}, s32[]{}, /*index=10*/s32[]{}) while((s32[]{:T(128)}, f32[16,6,512]{2,1,0:T(8,128)}, f32[16,7,512]{2,1,0:T(8,128)}, s32[]{:T(128)}, s32[]{:T(128)}, /*index=5*/s32[]{}, s32[]{}, ...), condition=%wide.region_10.11_spmd, body=%wide.region_0.10_spmd.sunk | while | flops 12850184 | bytes 152273 | solution.py:90
  (928 shorter events, 283.4 us)
Async XLA Ops:
  0.6 19.9 %collective-permute-start = (f32[7,16,512]{2,0,1:T(8,128)}, f32[7,16,512]{2,0,1:T(8,128)S(1)}, u32[]{:S(2)}, u32[]{:S(2)}) collective-permute-start(f32[7,16,512]{2,0,1:T(8,128)} %bitcast.292), channel_id=1, source_target_pairs={{0,3},{1,4},{2,5},{3,6},{4,7},{5,8},{6,9},{7,10},{8,11},{9,12},{10... | collective-permute-start | bytes 688136 | tf_op jit(solution)/shard_map/ppermute | solution.py:16
  6.0 17.4 %collective-permute-start.1 = (f32[7,16,512]{2,0,1:T(8,128)}, f32[7,16,512]{2,0,1:T(8,128)S(1)}, u32[]{:S(2)}, u32[]{:S(2)}) collective-permute-start(f32[7,16,512]{2,0,1:T(8,128)} %bitcast.293), channel_id=1, source_target_pairs={{0,2},{1,3},{2,4},{3,5},{4,6},{5,7},{6,8},{7,9},{8,10},{9,11},{10,... | collective-permute-start | bytes 688136 | tf_op jit(solution)/shard_map/ppermute | solution.py:16
  8.3 15.1 %collective-permute-start.2 = (f32[7,16,512]{2,0,1:T(8,128)}, f32[7,16,512]{2,0,1:T(8,128)S(1)}, u32[]{:S(2)}, u32[]{:S(2)}) collective-permute-start(f32[7,16,512]{2,0,1:T(8,128)} %bitcast.294), channel_id=1, source_target_pairs={{0,1},{1,2},{2,3},{3,4},{4,5},{5,6},{6,7},{7,8},{8,9},{9,10},{10,1... | collective-permute-start | bytes 688136 | tf_op jit(solution)/shard_map/ppermute | solution.py:16
  10.5 13.9 %collective-permute-start.3 = (f32[7,16,512]{2,0,1:T(8,128)}, f32[7,16,512]{2,0,1:T(8,128)S(1)}, u32[]{:S(2)}, u32[]{:S(2)}) collective-permute-start(f32[7,16,512]{2,0,1:T(8,128)} %bitcast.295), channel_id=1, source_target_pairs={{1,0},{2,1},{3,2},{4,3},{5,4},{6,5},{7,6},{8,7},{9,8},{10,9},{11,1... | collective-permute-start | bytes 688136 | tf_op jit(solution)/shard_map/ppermute | solution.py:16
  12.7 14.2 %collective-permute-start.4 = (f32[7,16,512]{2,0,1:T(8,128)}, f32[7,16,512]{2,0,1:T(8,128)S(1)}, u32[]{:S(2)}, u32[]{:S(2)}) collective-permute-start(f32[7,16,512]{2,0,1:T(8,128)} %bitcast.296), channel_id=1, source_target_pairs={{2,0},{3,1},{4,2},{5,3},{6,4},{7,5},{8,6},{9,7},{10,8},{11,9},{12,... | collective-permute-start | bytes 688136 | tf_op jit(solution)/shard_map/ppermute | solution.py:16
  20.6 14.1 %collective-permute-start.5 = (f32[7,16,512]{2,0,1:T(8,128)}, f32[7,16,512]{2,0,1:T(8,128)S(1)}, u32[]{:S(2)}, u32[]{:S(2)}) collective-permute-start(f32[7,16,512]{2,0,1:T(8,128)} %bitcast.297), channel_id=1, source_target_pairs={{3,0},{4,1},{5,2},{6,3},{7,4},{8,5},{9,6},{10,7},{11,8},{12,9},{13... | collective-permute-start | bytes 688136 | tf_op jit(solution)/shard_map/ppermute | solution.py:16
  24.4 11.7 %copy-start.1 = (s32[192,2]{0,1:T(2,128)S(1)}, s32[192,2]{0,1:T(2,128)}, u32[]{:S(2)}) copy-start(s32[192,2]{0,1:T(2,128)} %param.8) | copy-start | bytes 4612
  34.7 1.3 copy-start
  731.8 202.4 %collective-permute-start.10 = (f32[16,6,512]{2,1,0:T(8,128)}, f32[16,6,512]{2,1,0:T(8,128)S(1)}, u32[]{:S(2)}, u32[]{:S(2)}) collective-permute-start(f32[16,6,512]{2,1,0:T(8,128)} %get-tuple-element.146), channel_id=1, source_target_pairs={{0,2},{1,3},{2,4},{3,5},{4,6},{5,7},{6,8},{7,9},{8,10},{9,11},{10,... | collective-permute-start | bytes 589832 | tf_op jit(solution)/shard_map/ppermute | solution.py:16
  767.9 235.8 %collective-permute-start.11 = (f32[16,6,512]{2,1,0:T(8,128)}, f32[16,6,512]{2,1,0:T(8,128)S(1)}, u32[]{:S(2)}, u32[]{:S(2)}) collective-permute-start(f32[16,6,512]{2,1,0:T(8,128)} %get-tuple-element.145), channel_id=1, source_target_pairs={{0,3},{1,4},{2,5},{3,6},{4,7},{5,8},{6,9},{7,10},{8,11},{9,12},{10... | collective-permute-start | bytes 589832 | tf_op jit(solution)/shard_map/ppermute | solution.py:16
  847.9 155.8 %collective-permute-start.6 = (f32[16,6,512]{2,1,0:T(8,128)}, f32[16,6,512]{2,1,0:T(8,128)S(1)}, u32[]{:S(2)}, u32[]{:S(2)}) collective-permute-start(f32[16,6,512]{2,1,0:T(8,128)} %get-tuple-element.144), channel_id=1, source_target_pairs={{3,0},{4,1},{5,2},{6,3},{7,4},{8,5},{9,6},{10,7},{11,8},{12,9},{13... | collective-permute-start | bytes 589832 | tf_op jit(solution)/shard_map/ppermute | solution.py:16
  854.5 149.2 %collective-permute-start.7 = (f32[16,6,512]{2,1,0:T(8,128)S(1)}, f32[16,6,512]{2,1,0:T(8,128)}, u32[]{:S(2)}, u32[]{:S(2)}) collective-permute-start(f32[16,6,512]{2,1,0:T(8,128)S(1)} %get-tuple-element.149), channel_id=1, source_target_pairs={{2,0},{3,1},{4,2},{5,3},{6,4},{7,5},{8,6},{9,7},{10,8},{11,9},{12,... | collective-permute-start | bytes 589832 | tf_op jit(solution)/shard_map/ppermute | solution.py:16
  885.5 118.2 %collective-permute-start.8 = (f32[16,6,512]{2,1,0:T(8,128)S(1)}, f32[16,6,512]{2,1,0:T(8,128)}, u32[]{:S(2)}, u32[]{:S(2)}) collective-permute-start(f32[16,6,512]{2,1,0:T(8,128)S(1)} %get-tuple-element.148), channel_id=1, source_target_pairs={{1,0},{2,1},{3,2},{4,3},{5,4},{6,5},{7,6},{8,7},{9,8},{10,9},{11,1... | collective-permute-start | bytes 589832 | tf_op jit(solution)/shard_map/ppermute | solution.py:16
  934.3 69.5 %collective-permute-start.9 = (f32[16,6,512]{2,1,0:T(8,128)S(1)}, f32[16,6,512]{2,1,0:T(8,128)}, u32[]{:S(2)}, u32[]{:S(2)}) collective-permute-start(f32[16,6,512]{2,1,0:T(8,128)S(1)} %get-tuple-element.147), channel_id=1, source_target_pairs={{0,1},{1,2},{2,3},{3,4},{4,5},{5,6},{6,7},{7,8},{8,9},{9,10},{10,1... | collective-permute-start | bytes 589832 | tf_op jit(solution)/shard_map/ppermute | solution.py:16
where the time goes:
time: 1010 us
  other arithmetic  659 us (65%)
  starting transfers between devices  226 us (22%)
  local copies, waits for them, and re-layouts  102 us (10%)
  waiting for transfers between devices  10.2 us (1%)
    reduce_sum x19, other arithmetic, interact(): jnp.sum(steep * proj_second * cross_first[c], 0)  547 us
    ppermute x12, starting transfers between devices, passed_along(): lax.ppermute(value, axis, [(source, source + steps) for source in range(f...  226 us
    reduce_sum x16, other arithmetic, one_side(): jnp.sum(steep * proj_target * cross_source[c], 1)  40.6 us
    gather x19, local copies, waits for them, and re-layouts, visit(): window_rows[second_id]  39 us
    gather x19, local copies, waits for them, and re-layouts, visit(): window_rows[first_id]  39 us
  transfers between devices with their start and end apart: 12, of which 2 were waited for; matrix products, arithmetic and copies ran while one was open for 7% of the time, Pallas kernels for 0%

commit v1 on v0

v1 whole, which is shorter than its diff:
```python
import jax
import jax.numpy as jnp
from jax import lax
from jax.experimental import pallas as pl
from jax.experimental.pallas import tpu as pltpu
from jax.sharding import PartitionSpec as P

CLUSTER = 512
REACH = 3
BATCH = 8
ROWS = 8
SUMS = 27
PADDED = 32
LANES = CLUSTER // 128
inv_four_pi = 0.07957747154594767
f32 = jnp.float32
bf16 = jnp.bfloat16


def passed_along(value, axis, steps):
    count = lax.axis_size(axis)
    first, last = (max(0, -steps), min(count, count - steps))
    return lax.ppermute(value, axis, [(source, source + steps) for source in range(first, last)])


def cross_list(left, right):
    return [
        left[1] * right[2] - left[2] * right[1],
        left[2] * right[0] - left[0] * right[2],
        left[0] * right[1] - left[1] * right[0],
    ]


def aligned(index, size):
    return pl.ds(pl.multiple_of(index * size, size), size)


def wide(ref, rows):
    return jnp.concatenate([ref[lane, rows, :] for lane in range(LANES)], axis=1)


def put(ref, rows, value):
    for lane in range(LANES):
        ref[lane, rows, :] = value[:, lane * 128 : lane * 128 + 128]


def prepare(window, block, here, table, centres, columns, moments, sources):
    x = [window[block, c] for c in range(3)]
    a = [window[block, 3 + c] for c in range(3)]
    core = window[block, 6]
    half = 0.5 * core * core
    middle = [jnp.mean(x[c], axis=1, keepdims=True) for c in range(3)]
    y = [x[c] - middle[c] for c in range(3)]
    first = block * here * ROWS
    for k, plane in enumerate([x[0], x[1], x[2], half, a[0], a[1], a[2], jnp.zeros_like(half)]):
        put(table, pl.ds(first + k, here, stride=ROWS), plane)
    for k in range(3):
        centres[pl.ds(first + k, here, stride=ROWS), :] = jnp.broadcast_to(middle[k], (here, 128))
    b = cross_list(y, a)
    size = y[0] * y[0] + y[1] * y[1] + y[2] * y[2] + half
    planes = a + [y[d] * a[c] for d in range(3) for c in range(3)]
    planes += [y[d] * b[c] for d in range(3) for c in range(3)]
    planes += [size * a[c] for c in range(3)] + [size * b[c] for c in range(3)]
    for k, plane in enumerate(planes):
        put(moments, pl.ds(k, here, stride=PADDED), plane)

    def split(index, _):
        cluster = block * here + index
        whole = wide(moments, aligned(index, PADDED))
        for part in range(3):
            piece = whole.astype(bf16)
            sources[cluster, part * PADDED : (part + 1) * PADDED, :] = piece
            whole = whole - piece.astype(f32)
        columns[cluster] = wide(table, aligned(cluster, ROWS)).T
        return 0

    lax.fori_loop(0, here, split, 0)


def steepness(target, source, table, columns, high, low, own):
    step = 128
    second = wide(table, aligned(source, ROWS))
    for row in range(0, CLUSTER, step):
        column = columns[target, row : row + step, :]
        radial = [column[:, c : c + 1] - second[c : c + 1, :] for c in range(3)]
        spread = column[:, 3:4] + second[3:4, :]
        rho = radial[0] * radial[0] + radial[1] * radial[1] + radial[2] * radial[2] + spread
        steep = jnp.exp2(-2.5 * jnp.log2(rho))
        if own:
            rows = lax.broadcasted_iota(jnp.int32, rho.shape, 0) + row
            steep = jnp.where(rows == lax.broadcasted_iota(jnp.int32, rho.shape, 1), 0.0, steep)
        piece = steep.astype(bf16)
        high[row : row + step, :] = piece
        low[row : row + step, :] = (steep - piece.astype(f32)).astype(bf16)


def matmul(left, right, side):
    return lax.dot_general(left, right, (((1,), (side,)), ((), ())), preferred_element_type=f32)


def folded(source, high, low, side):
    total = matmul(source, high, side) + matmul(source, low, side)
    return total[:PADDED] + total[PADDED : 2 * PADDED] + total[2 * PADDED :]


def combine(sums, targets, middles, answers):
    for lane in range(LANES):
        g = [sums[lane, pl.ds(k, BATCH, stride=PADDED), :] for k in range(SUMS)]
        t = [targets[lane, pl.ds(k, BATCH, stride=ROWS), :] for k in (0, 1, 2, 4, 5, 6, 3)]
        x = [t[c] - middles[pl.ds(c, BATCH, stride=ROWS), :] for c in range(3)]
        a = t[3:6]
        plain = g[0:3]
        ya = [g[3 + 3 * d : 6 + 3 * d] for d in range(3)]
        yb = [g[12 + 3 * d : 15 + 3 * d] for d in range(3)]
        b = [ya[1][2] - ya[2][1], ya[2][0] - ya[0][2], ya[0][1] - ya[1][0]]
        size = x[0] * x[0] + x[1] * x[1] + x[2] * x[2] + t[6]
        twice = [2.0 * x[c] for c in range(3)]

        def along(vector, matrix, c):
            return vector[0] * matrix[0][c] + vector[1] * matrix[1][c] + vector[2] * matrix[2][c]

        ka = [size * plain[c] + (g[21 + c] - along(twice, ya, c)) for c in range(3)]
        kb = [size * b[c] + (g[24 + c] - along(twice, yb, c)) for c in range(3)]
        project = a[0] * x[0] + a[1] * x[1] + a[2] * x[2]
        q = [project * plain[c] - along(a, ya, c) for c in range(3)]
        r = [project * b[c] - along(a, yb, c) for c in range(3)]
        turn = cross_list(a, ka)
        moved = cross_list(x, ka)
        tilt = cross_list(x, q)
        for c in range(3):
            answers[lane, pl.ds(c, BATCH, stride=ROWS), :] = -inv_four_pi * (moved[c] - kb[c])
            answers[lane, pl.ds(3 + c, BATCH, stride=ROWS), :] = -inv_four_pi * (
                turn[c] - 3.0 * (tilt[c] - r[c])
            )


def kernel(
    pairs, count, window, out,
    table, centres, columns, moments, sources, total,
    high0, low0, high1, low1, sums_first, sums_second, targets, middles, answers,
):
    blocks = window.shape[0]
    here = window.shape[2]
    moments[...] = jnp.zeros_like(moments)
    total[...] = jnp.zeros_like(total)
    answers[...] = jnp.zeros_like(answers)
    for block in range(blocks):
        prepare(window, block, here, table, centres, columns, moments, sources)
    high, low = (high0, high1), (low0, low1)

    def spread_out(target_of, source_of, sums, live_of):
        for slot in range(BATCH):
            targets[:, slot * ROWS : (slot + 1) * ROWS, :] = table[:, aligned(target_of(slot), ROWS), :]
            middles[slot * ROWS : (slot + 1) * ROWS, :] = centres[aligned(source_of(slot), ROWS), :]
        combine(sums, targets, middles, answers)
        for slot in range(BATCH):

            @pl.when(live_of(slot))
            def _():
                where = aligned(target_of(slot), ROWS)
                total[:, where, :] += answers[:, slot * ROWS : (slot + 1) * ROWS, :]

    def own_batch(batch, _):
        def own_pair(turn, _):
            for h in range(2):
                slot = turn * 2 + h
                cluster = REACH * here + batch * BATCH + slot
                steepness(cluster, cluster, table, columns, high[h], low[h], True)
                put(
                    sums_first,
                    aligned(slot, PADDED),
                    folded(sources[cluster], high[h][...], low[h][...], 0),
                )
            return 0

        lax.fori_loop(0, BATCH // 2, own_pair, 0)
        own = lambda slot: REACH * here + batch * BATCH + slot
        spread_out(own, own, sums_first, lambda slot: slot >= 0)
        return 0

    lax.fori_loop(0, here // BATCH, own_batch, 0)

    live = count[0]
    device = lax.axis_index(("gx", "gy"))
    anchor = (device - REACH) * here

    def chosen(unit, side):
        held = jnp.clip(unit, 0, live - 1)
        return jnp.clip(pairs[held, side] - anchor, 0, blocks * here - 1)

    def pair_batch(batch, _):
        def pair_turn(turn, _):
            base = batch * BATCH + turn * 2
            for h in range(2):
                steepness(
                    chosen(base + h, 0), chosen(base + h, 1), table, columns, high[h], low[h], False
                )
                before = base + h - 1
                slot = turn * 2 + h
                hi, lo = high[1 - h][...], low[1 - h][...]
                put(sums_second, aligned(slot, PADDED), folded(sources[chosen(before, 0)], hi, lo, 0))
                put(sums_first, aligned(slot, PADDED), folded(sources[chosen(before, 1)], hi, lo, 1))
            return 0

        lax.fori_loop(0, BATCH // 2, pair_turn, 0)
        unit = lambda slot: batch * BATCH + slot - 1
        alive = lambda slot: jnp.logical_and(unit(slot) >= 0, unit(slot) < live)
        one = lambda slot: chosen(unit(slot), 0)
        two = lambda slot: chosen(unit(slot), 1)
        spread_out(one, two, sums_first, alive)
        spread_out(two, one, sums_second, alive)
        return 0

    lax.fori_loop(0, (live + BATCH) // BATCH, pair_batch, 0)

    for block in range(blocks):
        for k in range(6):
            out[block, k] = wide(total, pl.ds(block * here * ROWS + k, here, stride=ROWS))


def near_field(window, pair_list, pair_count):
    blocks, _, here, _ = window.shape
    clusters = blocks * here
    square = pltpu.VMEM((CLUSTER, CLUSTER), bf16)
    return pl.pallas_call(
        kernel,
        out_shape=jax.ShapeDtypeStruct((blocks, 6, here, CLUSTER), f32),
        in_specs=[
            pl.BlockSpec(memory_space=pltpu.SMEM),
            pl.BlockSpec(memory_space=pltpu.SMEM),
            pl.BlockSpec(memory_space=pltpu.VMEM),
        ],
        out_specs=pl.BlockSpec(memory_space=pltpu.VMEM),
        scratch_shapes=[
            pltpu.VMEM((LANES, clusters * ROWS, 128), f32),
            pltpu.VMEM((clusters * ROWS, 128), f32),
            pltpu.VMEM((clusters, CLUSTER, ROWS), f32),
            pltpu.VMEM((LANES, here * PADDED, 128), f32),
            pltpu.VMEM((clusters, 3 * PADDED, CLUSTER), bf16),
            pltpu.VMEM((LANES, clusters * ROWS, 128), f32),
            square, square, square, square,
            pltpu.VMEM((LANES, BATCH * PADDED, 128), f32),
            pltpu.VMEM((LANES, BATCH * PADDED, 128), f32),
            pltpu.VMEM((LANES, BATCH * ROWS, 128), f32),
            pltpu.VMEM((BATCH * ROWS, 128), f32),
            pltpu.VMEM((LANES, BATCH * ROWS, 128), f32),
        ],
        compiler_params=pltpu.CompilerParams(vmem_limit_bytes=58 * 2**20),
        name="near_field",
    )(pair_list, pair_count, window)


def shards(particles, pair_list, pair_count):
    width = particles.shape[1]
    here = width // CLUSTER
    owned = particles.reshape(7, here, CLUSTER)
    axis = ("gx", "gy")
    around = {0: owned}
    for offset in list(range(-REACH, 0)) + list(range(1, REACH + 1)):
        around[offset] = passed_along(owned, axis, -offset)
    window = jnp.stack([around[offset] for offset in range(-REACH, REACH + 1)])
    pieces = near_field(window, pair_list, pair_count)
    result = pieces[REACH]
    for offset in list(range(-REACH, 0)) + list(range(1, REACH + 1)):
        result = result + passed_along(pieces[offset + REACH], axis, offset)
    final = result.reshape(6, width)
    return (final[:3], final[3:])


def solution(mesh):
    placed = (P(None, ("gx", "gy")), P(("gx", "gy"), None), P(("gx", "gy")))
    return jax.shard_map(
        shards,
        mesh=mesh,
        in_specs=placed,
        out_specs=(P(None, ("gx", "gy")), P(None, ("gx", "gy"))),
        check_vma=False,
    )
```

time: 1010 us -> 298 us (0.30)
  the two profiles are of different devices: /device:TPU:3 before, /device:TPU:6 now
where the time goes in v1:
time: 298 us; the launch traced here: 292 us
  Pallas kernels  225 us (76%)
  starting transfers between devices  42.6 us (14%)
  waiting for transfers between devices  15.1 us (5%)
  local copies, waits for them, and re-layouts  6.95 us (2%)
    pallas_call x1, Pallas kernels, near_field(): pl.pallas_call(kernel, out_shape=jax.ShapeDtypeStruct((blocks, 6, here, C...  225 us
    ppermute x12, starting transfers between devices, passed_along(): lax.ppermute(value, axis, [(source, source + steps) for source in range(f...  42.6 us
    ppermute x12, waiting for transfers between devices, passed_along(): lax.ppermute(value, axis, [(source, source + steps) for source in range(f...  15.1 us
  transfers between devices with their start and end apart: 12, of which 4 were waited for; matrix products, arithmetic and copies ran while one was open for 1% of the time, Pallas kernels for 0%

profile of v1, /device:TPU:6, one launch (start us, length us, event | category | flops | bytes accessed | tf_op | source)
XLA Modules:
  0.0 291.8 jit_solution(16734372979053868222)
XLA Ops:
  0.6 1.2 copy.12
  1.8 2.9 %collective-permute-start = (f32[7,16,512]{2,1,0:T(8,128)S(1)}, f32[7,16,512]{2,1,0:T(8,128)S(1)}, u32[]{:S(2)}, u32[]{:S(2)}) collective-permute-start(f32[7,16,512]{2,1,0:T(8,128)S(1)} %bitcast.54), channel_id=1, source_target_pairs={{0,3},{1,4},{2,5},{3,6},{4,7},{5,8},{6,9},{7,10},{8,11},{9,12},{10... | collective-permute-start | bytes 688136 | tf_op jit(solution)/shard_map/ppermute | solution.py:23
  4.7 3.5 %collective-permute-start.1 = (f32[7,16,512]{2,1,0:T(8,128)S(1)}, f32[7,16,512]{2,1,0:T(8,128)S(1)}, u32[]{:S(2)}, u32[]{:S(2)}) collective-permute-start(f32[7,16,512]{2,1,0:T(8,128)S(1)} %bitcast.55), channel_id=1, source_target_pairs={{0,2},{1,3},{2,4},{3,5},{4,6},{5,7},{6,8},{7,9},{8,10},{9,11},{10,... | collective-permute-start | bytes 688136 | tf_op jit(solution)/shard_map/ppermute | solution.py:23
  8.2 3.0 %collective-permute-start.2 = (f32[7,16,512]{2,1,0:T(8,128)S(1)}, f32[7,16,512]{2,1,0:T(8,128)S(1)}, u32[]{:S(2)}, u32[]{:S(2)}) collective-permute-start(f32[7,16,512]{2,1,0:T(8,128)S(1)} %bitcast.56), channel_id=1, source_target_pairs={{0,1},{1,2},{2,3},{3,4},{4,5},{5,6},{6,7},{7,8},{8,9},{9,10},{10,1... | collective-permute-start | bytes 688136 | tf_op jit(solution)/shard_map/ppermute | solution.py:23
  11.2 7.1 %collective-permute-start.3 = (f32[7,16,512]{2,1,0:T(8,128)S(1)}, f32[7,16,512]{2,1,0:T(8,128)S(1)}, u32[]{:S(2)}, u32[]{:S(2)}) collective-permute-start(f32[7,16,512]{2,1,0:T(8,128)S(1)} %bitcast.57), channel_id=1, source_target_pairs={{1,0},{2,1},{3,2},{4,3},{5,4},{6,5},{7,6},{8,7},{9,8},{10,9},{11,1... | collective-permute-start | bytes 688136 | tf_op jit(solution)/shard_map/ppermute | solution.py:23
  18.3 2.3 collective-permute-start.4
  20.7 1.4 copy.5.pairs
  22.8 2.3 collective-permute-start.5
  25.4 1.7 collective-permute-done.4
  27.1 4.6 %collective-permute-done.5 = f32[7,16,512]{2,1,0:T(8,128)S(1)} collective-permute-done((f32[7,16,512]{2,1,0:T(8,128)S(1)}, f32[7,16,512]{2,1,0:T(8,128)S(1)}, u32[]{:S(2)}, u32[]{:S(2)}) %collective-permute-start.5) | collective-permute-done | bytes 229408 | tf_op jit(solution)/shard_map/ppermute | solution.py:23
  31.7 1.2 copy-done
  32.9 224.6 %near_field.1 = f32[7,6,16,512]{3,2,1,0:T(8,128)} custom-call(s32[192,2]{1,0:T(8,128)} %copy.5.pairs, s32[1]{0:T(128)S(6)} %copy.19.count, f32[7,7,16,512]{3,2,1,0:T(8,128)} %copy-done), custom_call_target="tpu_custom_call" | custom-call | tf_op jit(solution)/shard_map/near_field/pallas_call | solution.py:225
  257.5 1.5 slice_bitcast_fusion.5
  258.9 1.9 collective-permute-start.10
  260.9 1.9 collective-permute-start.11
  262.8 8.2 %collective-permute-start.6 = (f32[6,16,512]{2,1,0:T(8,128)S(1)}, f32[6,16,512]{2,1,0:T(8,128)S(1)}, u32[]{:S(2)}, u32[]{:S(2)}) collective-permute-start(f32[6,16,512]{2,1,0:T(8,128)S(1)} %get-tuple-element.2), channel_id=1, source_target_pairs={{3,0},{4,1},{5,2},{6,3},{7,4},{8,5},{9,6},{10,7},{11,8},{12,9},{13... | collective-permute-start | bytes 589832 | tf_op jit(solution)/shard_map/ppermute | solution.py:23
  271.0 5.1 %collective-permute-start.7 = (f32[6,16,512]{2,1,0:T(8,128)S(1)}, f32[6,16,512]{2,1,0:T(8,128)S(1)}, u32[]{:S(2)}, u32[]{:S(2)}) collective-permute-start(f32[6,16,512]{2,1,0:T(8,128)S(1)} %get-tuple-element.7), channel_id=1, source_target_pairs={{2,0},{3,1},{4,2},{5,3},{6,4},{7,5},{8,6},{9,7},{10,8},{11,9},{12,... | collective-permute-start | bytes 589832 | tf_op jit(solution)/shard_map/ppermute | solution.py:23
  276.1 1.9 collective-permute-start.8
  278.0 2.4 collective-permute-start.9
  280.5 1.5 collective-permute-done.8
  282.0 7.3 %collective-permute-done.9 = f32[6,16,512]{2,1,0:T(8,128)S(1)} collective-permute-done((f32[6,16,512]{2,1,0:T(8,128)S(1)}, f32[6,16,512]{2,1,0:T(8,128)S(1)}, u32[]{:S(2)}, u32[]{:S(2)}) %collective-permute-start.9) | collective-permute-done | bytes 196640 | tf_op jit(solution)/shard_map/ppermute | solution.py:23
  289.3 1.1 fusion.5
  290.3 0.7 copy.8
  291.1 0.7 copy.9
  (19 shorter events, 0.3 us)
Async XLA Ops:
  0.6 24.6 %copy-start.1 = (f32[7,8192]{1,0:T(8,128)S(1)}, f32[7,8192]{1,0:T(8,128)}, u32[]{:S(2)}) copy-start(f32[7,8192]{1,0:T(8,128)} %param.3) | copy-start | bytes 688132
  1.8 21.0 %collective-permute-start = (f32[7,16,512]{2,1,0:T(8,128)S(1)}, f32[7,16,512]{2,1,0:T(8,128)S(1)}, u32[]{:S(2)}, u32[]{:S(2)}) collective-permute-start(f32[7,16,512]{2,1,0:T(8,128)S(1)} %bitcast.54), channel_id=1, source_target_pairs={{0,3},{1,4},{2,5},{3,6},{4,7},{5,8},{6,9},{7,10},{8,11},{9,12},{10... | collective-permute-start | bytes 688136 | tf_op jit(solution)/shard_map/ppermute | solution.py:23
  4.7 20.4 %collective-permute-start.1 = (f32[7,16,512]{2,1,0:T(8,128)S(1)}, f32[7,16,512]{2,1,0:T(8,128)S(1)}, u32[]{:S(2)}, u32[]{:S(2)}) collective-permute-start(f32[7,16,512]{2,1,0:T(8,128)S(1)} %bitcast.55), channel_id=1, source_target_pairs={{0,2},{1,3},{2,4},{3,5},{4,6},{5,7},{6,8},{7,9},{8,10},{9,11},{10,... | collective-permute-start | bytes 688136 | tf_op jit(solution)/shard_map/ppermute | solution.py:23
  8.2 17.0 %collective-permute-start.2 = (f32[7,16,512]{2,1,0:T(8,128)S(1)}, f32[7,16,512]{2,1,0:T(8,128)S(1)}, u32[]{:S(2)}, u32[]{:S(2)}) collective-permute-start(f32[7,16,512]{2,1,0:T(8,128)S(1)} %bitcast.56), channel_id=1, source_target_pairs={{0,1},{1,2},{2,3},{3,4},{4,5},{5,6},{6,7},{7,8},{8,9},{9,10},{10,1... | collective-permute-start | bytes 688136 | tf_op jit(solution)/shard_map/ppermute | solution.py:23
  11.2 14.1 %collective-permute-start.3 = (f32[7,16,512]{2,1,0:T(8,128)S(1)}, f32[7,16,512]{2,1,0:T(8,128)S(1)}, u32[]{:S(2)}, u32[]{:S(2)}) collective-permute-start(f32[7,16,512]{2,1,0:T(8,128)S(1)} %bitcast.57), channel_id=1, source_target_pairs={{1,0},{2,1},{3,2},{4,3},{5,4},{6,5},{7,6},{8,7},{9,8},{10,9},{11,1... | collective-permute-start | bytes 688136 | tf_op jit(solution)/shard_map/ppermute | solution.py:23
  18.3 8.7 %collective-permute-start.4 = (f32[7,16,512]{2,1,0:T(8,128)S(1)}, f32[7,16,512]{2,1,0:T(8,128)S(1)}, u32[]{:S(2)}, u32[]{:S(2)}) collective-permute-start(f32[7,16,512]{2,1,0:T(8,128)S(1)} %bitcast.58), channel_id=1, source_target_pairs={{2,0},{3,1},{4,2},{5,3},{6,4},{7,5},{8,6},{9,7},{10,8},{11,9},{12,... | collective-permute-start | bytes 688136 | tf_op jit(solution)/shard_map/ppermute | solution.py:23
  22.8 8.9 %collective-permute-start.5 = (f32[7,16,512]{2,1,0:T(8,128)S(1)}, f32[7,16,512]{2,1,0:T(8,128)S(1)}, u32[]{:S(2)}, u32[]{:S(2)}) collective-permute-start(f32[7,16,512]{2,1,0:T(8,128)S(1)} %bitcast.59), channel_id=1, source_target_pairs={{3,0},{4,1},{5,2},{6,3},{7,4},{8,5},{9,6},{10,7},{11,8},{12,9},{13... | collective-permute-start | bytes 688136 | tf_op jit(solution)/shard_map/ppermute | solution.py:23
  31.7 1.2 copy-start
  258.9 19.1 %collective-permute-start.10 = (f32[6,16,512]{2,1,0:T(8,128)S(1)}, f32[6,16,512]{2,1,0:T(8,128)S(1)}, u32[]{:S(2)}, u32[]{:S(2)}) collective-permute-start(f32[6,16,512]{2,1,0:T(8,128)S(1)} %get-tuple-element.4), channel_id=1, source_target_pairs={{0,2},{1,3},{2,4},{3,5},{4,6},{5,7},{6,8},{7,9},{8,10},{9,11},{10,... | collective-permute-start | bytes 589832 | tf_op jit(solution)/shard_map/ppermute | solution.py:23
  260.9 19.6 %collective-permute-start.11 = (f32[6,16,512]{2,1,0:T(8,128)S(1)}, f32[6,16,512]{2,1,0:T(8,128)S(1)}, u32[]{:S(2)}, u32[]{:S(2)}) collective-permute-start(f32[6,16,512]{2,1,0:T(8,128)S(1)} %get-tuple-element.3), channel_id=1, source_target_pairs={{0,3},{1,4},{2,5},{3,6},{4,7},{5,8},{6,9},{7,10},{8,11},{9,12},{10... | collective-permute-start | bytes 589832 | tf_op jit(solution)/shard_map/ppermute | solution.py:23
  262.8 17.7 %collective-permute-start.6 = (f32[6,16,512]{2,1,0:T(8,128)S(1)}, f32[6,16,512]{2,1,0:T(8,128)S(1)}, u32[]{:S(2)}, u32[]{:S(2)}) collective-permute-start(f32[6,16,512]{2,1,0:T(8,128)S(1)} %get-tuple-element.2), channel_id=1, source_target_pairs={{3,0},{4,1},{5,2},{6,3},{7,4},{8,5},{9,6},{10,7},{11,8},{12,9},{13... | collective-permute-start | bytes 589832 | tf_op jit(solution)/shard_map/ppermute | solution.py:23
  271.0 9.5 %collective-permute-start.7 = (f32[6,16,512]{2,1,0:T(8,128)S(1)}, f32[6,16,512]{2,1,0:T(8,128)S(1)}, u32[]{:S(2)}, u32[]{:S(2)}) collective-permute-start(f32[6,16,512]{2,1,0:T(8,128)S(1)} %get-tuple-element.7), channel_id=1, source_target_pairs={{2,0},{3,1},{4,2},{5,3},{6,4},{7,5},{8,6},{9,7},{10,8},{11,9},{12,... | collective-permute-start | bytes 589832 | tf_op jit(solution)/shard_map/ppermute | solution.py:23
  276.1 5.9 %collective-permute-start.8 = (f32[6,16,512]{2,1,0:T(8,128)S(1)}, f32[6,16,512]{2,1,0:T(8,128)S(1)}, u32[]{:S(2)}, u32[]{:S(2)}) collective-permute-start(f32[6,16,512]{2,1,0:T(8,128)S(1)} %get-tuple-element.6), channel_id=1, source_target_pairs={{1,0},{2,1},{3,2},{4,3},{5,4},{6,5},{7,6},{8,7},{9,8},{10,9},{11,1... | collective-permute-start | bytes 589832 | tf_op jit(solution)/shard_map/ppermute | solution.py:23
  278.0 11.2 %collective-permute-start.9 = (f32[6,16,512]{2,1,0:T(8,128)S(1)}, f32[6,16,512]{2,1,0:T(8,128)S(1)}, u32[]{:S(2)}, u32[]{:S(2)}) collective-permute-start(f32[6,16,512]{2,1,0:T(8,128)S(1)} %get-tuple-element.5), channel_id=1, source_target_pairs={{0,1},{1,2},{2,3},{3,4},{4,5},{5,6},{6,7},{7,8},{8,9},{9,10},{10,1... | collective-permute-start | bytes 589832 | tf_op jit(solution)/shard_map/ppermute | solution.py:23

commit v2 on v0

v2 whole, which is shorter than its diff:
```python
import functools

import jax
import jax.numpy as jnp
from jax import lax
from jax.experimental import pallas as pl
from jax.experimental.pallas import tpu as pltpu
from jax.sharding import PartitionSpec as P

CLUSTER = 512
REACH = 3
BATCH = 8
ROWS = 8
SUMS = 27
STRIP = 128
PADDED = 32
LANES = CLUSTER // 128
inv_four_pi = 0.07957747154594767
f32 = jnp.float32
bf16 = jnp.bfloat16


def passed_along(value, axis, steps):
    count = lax.axis_size(axis)
    first, last = (max(0, -steps), min(count, count - steps))
    return lax.ppermute(value, axis, [(source, source + steps) for source in range(first, last)])


def cross_list(left, right):
    return [
        left[1] * right[2] - left[2] * right[1],
        left[2] * right[0] - left[0] * right[2],
        left[0] * right[1] - left[1] * right[0],
    ]


def aligned(index, size):
    return pl.ds(pl.multiple_of(index * size, size), size)


def wide(ref, rows):
    return jnp.concatenate([ref[lane, rows, :] for lane in range(LANES)], axis=1)


def put(ref, rows, value, *lead):
    for lane in range(LANES):
        ref[(*lead, lane, rows, slice(None))] = value[:, lane * 128 : lane * 128 + 128]


def prepare(window, block, here, table, centres, moments, sources):
    x = [window[block, c] for c in range(3)]
    a = [window[block, 3 + c] for c in range(3)]
    core = window[block, 6]
    half = 0.5 * core * core
    middle = [jnp.mean(x[c], axis=1, keepdims=True) for c in range(3)]
    y = [x[c] - middle[c] for c in range(3)]
    first = block * here * ROWS
    for k, plane in enumerate([x[0], x[1], x[2], half, a[0], a[1], a[2], jnp.zeros_like(half)]):
        put(table, pl.ds(first + k, here, stride=ROWS), plane)
    for k in range(3):
        centres[pl.ds(first + k, here, stride=ROWS), :] = jnp.broadcast_to(middle[k], (here, 128))
    b = cross_list(y, a)
    size = y[0] * y[0] + y[1] * y[1] + y[2] * y[2] + half
    planes = a + [y[d] * a[c] for d in range(3) for c in range(3)]
    planes += [y[d] * b[c] for d in range(3) for c in range(3)]
    planes += [size * a[c] for c in range(3)] + [size * b[c] for c in range(3)]
    for k, plane in enumerate(planes):
        put(moments, pl.ds(k, here, stride=PADDED), plane)

    def split(turn, _):
        for index in [turn * 4 + k for k in range(4)]:
            whole = wide(moments, aligned(index, PADDED))
            for part in range(3):
                piece = whole.astype(bf16)
                sources[block * here + index, part * PADDED : (part + 1) * PADDED, :] = piece
                whole = whole - piece.astype(f32)
        return 0

    lax.fori_loop(0, here // 4, split, 0)


def parted(rows):
    high = rows.astype(bf16).astype(f32)
    rest = rows - high
    middle = rest.astype(bf16).astype(f32)
    return high, middle, rest - middle


def features(rows, middle, left):
    place = lax.broadcasted_iota(jnp.int32, rows.shape, 0)
    moved = rows - jnp.concatenate([middle] * LANES, axis=1)
    size = jnp.where(place < 3, moved * moved, jnp.where(place == 3, moved, 0.0))
    size = jnp.sum(size, axis=0, keepdims=True)
    if left:
        whole = jnp.where(place < 3, moved, jnp.where(place == 3, size, jnp.where(place == 4, 1.0, 0.0)))
        h, m, l = parted(whole)
        return jnp.concatenate([h, h, m, m, h, l], axis=0)
    whole = jnp.where(place < 3, -2.0 * moved, jnp.where(place == 3, 1.0, jnp.where(place == 4, size, 0.0)))
    h, m, l = parted(whole)
    return jnp.concatenate([h, m, h, m, l, h], axis=0)


def steepness(target, source, table, centres, high, low, high_across=None, low_across=None):
    step = STRIP
    second = wide(table, aligned(source, ROWS))
    middle = centres[aligned(target, ROWS), :]
    left = features(wide(table, aligned(target, ROWS)), middle, True).T.astype(bf16)
    right = features(second, middle, False).astype(bf16)
    for row in range(0, CLUSTER, step):
        rho = jnp.maximum(matmul(left[row : row + step], right), second[3:4, :])
        inverse = lax.rsqrt(rho)
        square = inverse * inverse
        steep = square * square * inverse
        if high_across is None:
            rows = lax.broadcasted_iota(jnp.int32, rho.shape, 0) + row
            steep = jnp.where(rows == lax.broadcasted_iota(jnp.int32, rho.shape, 1), 0.0, steep)
        piece = steep.astype(bf16)
        rest = (steep - piece.astype(f32)).astype(bf16)
        high[row : row + step, :] = piece
        low[row : row + step, :] = rest
        if high_across is not None:
            high_across[:, row : row + step] = piece.T
            low_across[:, row : row + step] = rest.T


def matmul(left, right):
    return lax.dot_general(left, right, (((1,), (0,)), ((), ())), preferred_element_type=f32)


def folded(source, high, low):
    total = matmul(source, high) + matmul(source, low)
    return total[:PADDED] + total[PADDED : 2 * PADDED] + total[2 * PADDED :]


def combine(sums, parity, lane, targets, middles, answers):
    g = [sums[parity, lane, pl.ds(k, BATCH, stride=PADDED), :] for k in range(SUMS)]
    t = [targets[pl.ds(k, BATCH, stride=ROWS), :] for k in (0, 1, 2, 4, 5, 6, 3)]
    x = [t[c] - middles[pl.ds(c, BATCH, stride=ROWS), :] for c in range(3)]
    a = t[3:6]
    plain = g[0:3]
    ya = [g[3 + 3 * d : 6 + 3 * d] for d in range(3)]
    yb = [g[12 + 3 * d : 15 + 3 * d] for d in range(3)]
    b = [ya[1][2] - ya[2][1], ya[2][0] - ya[0][2], ya[0][1] - ya[1][0]]
    size = x[0] * x[0] + x[1] * x[1] + x[2] * x[2] + t[6]
    twice = [2.0 * x[c] for c in range(3)]

    def along(vector, matrix, c):
        return vector[0] * matrix[0][c] + vector[1] * matrix[1][c] + vector[2] * matrix[2][c]

    ka = [size * plain[c] + (g[21 + c] - along(twice, ya, c)) for c in range(3)]
    kb = [size * b[c] + (g[24 + c] - along(twice, yb, c)) for c in range(3)]
    project = a[0] * x[0] + a[1] * x[1] + a[2] * x[2]
    q = [project * plain[c] - along(a, ya, c) for c in range(3)]
    r = [project * b[c] - along(a, yb, c) for c in range(3)]
    turn = cross_list(a, ka)
    moved = cross_list(x, ka)
    tilt = cross_list(x, q)
    for c in range(3):
        answers[pl.ds(c, BATCH, stride=ROWS), :] = -inv_four_pi * (moved[c] - kb[c])
        answers[pl.ds(3 + c, BATCH, stride=ROWS), :] = -inv_four_pi * (
            turn[c] - 3.0 * (tilt[c] - r[c])
        )


def settle(target_of, source_of, live_of, sums, parity, lane, table, centres, total, room):
    targets, middles, answers = room
    for slot in range(BATCH):
        targets[slot * ROWS : (slot + 1) * ROWS, :] = table[lane, aligned(target_of(slot), ROWS), :]
        middles[slot * ROWS : (slot + 1) * ROWS, :] = centres[aligned(source_of(slot), ROWS), :]
    combine(sums, parity, lane, targets, middles, answers)
    for slot in range(BATCH):
        update = answers[slot * ROWS : (slot + 1) * ROWS, :]
        if live_of is not None:
            update = jnp.where(live_of(slot), update, 0.0)
        total[lane, aligned(target_of(slot), ROWS), :] += update


def begin(window, table, centres, moments, sources, total):
    blocks, _, here, _ = window.shape
    moments[...] = jnp.zeros_like(moments)
    centres[...] = jnp.zeros_like(centres)
    total[...] = jnp.zeros_like(total)
    for block in range(blocks):
        prepare(window, block, here, table, centres, moments, sources)


def finish(total, out):
    blocks, _, here, _ = out.shape
    for block in range(blocks):
        for k in range(6):
            out[block, k] = wide(total, pl.ds(block * here * ROWS + k, here, stride=ROWS))


def own_kernel(
    pairs, count, start, window, out, order, bounds,
    table, centres, moments, sources, total, high0, low0, high1, low1, sums, targets, middles, answers,
):
    here = window.shape[2]
    live = count[0]
    anchor = start[0]
    last = (2 * REACH + 1) * here - 1

    def place(slot, front):
        first = jnp.clip(pairs[slot, 0] - anchor, 0, last)
        second = jnp.clip(pairs[slot, 1] - anchor, 0, last)
        inner = jnp.logical_and(first >= REACH * here, second < (REACH + 1) * here)
        inner = jnp.logical_and(inner, jnp.logical_and(second >= REACH * here, first < (REACH + 1) * here))
        where = jnp.where(inner, live - 1 - (slot - front), front)
        order[where, 0] = first
        order[where, 1] = second
        return front + jnp.where(inner, 0, 1)

    bounds[0] = lax.fori_loop(0, live, place, 0)
    bounds[1] = live
    begin(window, table, centres, moments, sources, total)
    answers[...] = jnp.zeros_like(answers)
    high, low = (high0, high1), (low0, low1)
    steepness(0, 0, table, centres, high0, low0)

    def own_turn(turn, _):
        for h in range(2):
            cluster = turn * 2 + h
            following = jnp.minimum(cluster + 1, here - 1)
            steepness(following, following, table, centres, high[1 - h], low[1 - h])
            answer = folded(sources[cluster], high[h][...], low[h][...])
            put(sums, aligned(lax.rem(cluster, BATCH), PADDED), answer, lax.div(cluster, BATCH))
        return 0

    lax.fori_loop(0, here // 2, own_turn, 0)

    def own_settle(batch, _):
        own = lambda slot: batch * BATCH + slot
        for lane in range(LANES):
            settle(own, own, None, sums, batch, lane, table, centres, total, (targets, middles, answers))
        return 0

    lax.fori_loop(0, here // BATCH, own_settle, 0)
    finish(total, out)


def pair_kernel(
    shift, inner, order, bounds, window, out,
    table, centres, moments, sources, total, high0, low0, high1, low1,
    high_across0, low_across0, high_across1, low_across1, sums_first, sums_second, *rooms,
):
    blocks, _, here, _ = window.shape
    begin(window, table, centres, moments, sources, total)
    room_first, room_second = rooms[:3], rooms[3:]
    for room in (room_first, room_second):
        room[2][...] = jnp.zeros_like(room[2])
    for square in (high1, low1, high_across1, low_across1):
        square[...] = jnp.zeros_like(square)
    squares = (
        (high0, low0, high_across0, low_across0),
        (high1, low1, high_across1, low_across1),
    )
    first_unit = bounds[0] if inner else 0
    end_unit = bounds[1] if inner else bounds[0]

    def chosen(unit, side):
        held = jnp.maximum(jnp.clip(unit, first_unit, end_unit - 1), 0)
        return jnp.clip(order[held, side] - shift, 0, blocks * here - 1)

    def settle_part(turn):
        batch = lax.div(turn, BATCH // 2) - 1
        lane = lax.rem(turn, BATCH // 2)
        parity = lax.rem(batch + 2, 2)
        unit = lambda slot: first_unit + batch * BATCH + slot - 1
        alive = lambda slot: jnp.logical_and(unit(slot) >= first_unit, unit(slot) < end_unit)
        one = lambda slot: chosen(unit(slot), 0)
        two = lambda slot: chosen(unit(slot), 1)
        settle(one, two, alive, sums_first, parity, lane, table, centres, total, room_first)
        settle(two, one, alive, sums_second, parity, lane, table, centres, total, room_second)

    def pair_turn(turn, _):
        base = first_unit + turn * 2
        parity = lax.rem(lax.div(turn, BATCH // 2), 2)
        for h in range(2):
            steepness(chosen(base + h, 0), chosen(base + h, 1), table, centres, *squares[h])
            before = base + h - 1
            rows = aligned(lax.rem(turn, BATCH // 2) * 2 + h, PADDED)
            hi, lo, hi_across, lo_across = [ref[...] for ref in squares[1 - h]]
            put(sums_second, rows, folded(sources[chosen(before, 0)], hi, lo), parity)
            put(sums_first, rows, folded(sources[chosen(before, 1)], hi_across, lo_across), parity)
        settle_part(turn)
        return 0

    def settle_turn(turn, _):
        settle_part(turn)
        return 0

    turns = lax.div(end_unit - first_unit + 2, 2)
    lax.fori_loop(0, turns, pair_turn, 0)
    quarter = BATCH // 2
    lax.fori_loop(turns, lax.div(turns + quarter - 1, quarter) * quarter + quarter, settle_turn, 0)
    finish(total, out)


def tables(clusters, here):
    return [
        pltpu.VMEM((LANES, clusters * ROWS, 128), f32),
        pltpu.VMEM((clusters * ROWS, 128), f32),
        pltpu.VMEM((LANES, here * PADDED, 128), f32),
        pltpu.VMEM((clusters, 3 * PADDED, CLUSTER), bf16),
        pltpu.VMEM((LANES, clusters * ROWS, 128), f32),
    ]


in_scalars = pl.BlockSpec(memory_space=pltpu.SMEM)
in_vectors = pl.BlockSpec(memory_space=pltpu.VMEM)
square = pltpu.VMEM((CLUSTER, CLUSTER), bf16)
room = [pltpu.VMEM((BATCH * ROWS, 128), f32)] * 3


def own_terms(owned, pair_list, pair_count, anchor):
    here = owned.shape[2]
    return pl.pallas_call(
        own_kernel,
        out_shape=[
            jax.ShapeDtypeStruct((1, 6, here, CLUSTER), f32),
            jax.ShapeDtypeStruct(pair_list.shape, jnp.int32),
            jax.ShapeDtypeStruct((2,), jnp.int32),
        ],
        in_specs=[in_scalars, in_scalars, in_scalars, in_vectors],
        out_specs=[in_vectors, in_scalars, in_scalars],
        scratch_shapes=tables(here, here)
        + [square] * 4
        + [pltpu.VMEM((here // BATCH, LANES, BATCH * PADDED, 128), f32)]
        + room,
        compiler_params=pltpu.CompilerParams(vmem_limit_bytes=32 * 2**20),
        cost_estimate=pl.CostEstimate(flops=12 * 10**9, bytes_accessed=10**6, transcendentals=0),
        name="own_terms",
    )(pair_list, pair_count, anchor, owned)


def pair_terms(window, order, bounds, inner):
    blocks, _, here, _ = window.shape
    clusters = blocks * here
    sums = pltpu.VMEM((2, LANES, BATCH * PADDED, 128), f32)
    return pl.pallas_call(
        functools.partial(pair_kernel, REACH * here if inner else 0, inner),
        out_shape=jax.ShapeDtypeStruct((blocks, 6, here, CLUSTER), f32),
        in_specs=[in_scalars, in_scalars, in_vectors],
        out_specs=in_vectors,
        scratch_shapes=tables(clusters, here) + [square] * 8 + [sums] * 2 + room * 2,
        compiler_params=pltpu.CompilerParams(vmem_limit_bytes=50 * 2**20),
        cost_estimate=pl.CostEstimate(
            flops=(16 if inner else 150) * 10**9, bytes_accessed=10**6, transcendentals=0
        ),
        name="inner_pairs" if inner else "outer_pairs",
    )(order, bounds, window)


def shards(particles, pair_list, pair_count):
    width = particles.shape[1]
    here = width // CLUSTER
    owned = particles.reshape(7, here, CLUSTER)
    axis = ("gx", "gy")
    others = list(range(-REACH, 0)) + list(range(1, REACH + 1))
    around = {0: owned}
    for offset in others:
        around[offset] = passed_along(owned, axis, -offset)
    anchor = ((lax.axis_index(axis) - REACH) * here).astype(jnp.int32).reshape(1)
    alone, order, bounds = own_terms(owned[None], pair_list, pair_count, anchor)
    window = jnp.stack([around[offset] for offset in range(-REACH, REACH + 1)])
    pieces = pair_terms(window, order, bounds, False)
    inner = pair_terms(owned[None], order, bounds, True)
    result = alone[0] + inner[0] + pieces[REACH]
    for offset in others:
        result = result + passed_along(pieces[offset + REACH], axis, offset)
    final = result.reshape(6, width)
    return (final[:3], final[3:])


def solution(mesh):
    placed = (P(None, ("gx", "gy")), P(("gx", "gy"), None), P(("gx", "gy")))
    return jax.shard_map(
        shards,
        mesh=mesh,
        in_specs=placed,
        out_specs=(P(None, ("gx", "gy")), P(None, ("gx", "gy"))),
        check_vma=False,
    )
```

time: 1010 us -> 331 us (0.33)
  the two profiles are of different devices: /device:TPU:3 before, /device:TPU:127 now
where the time goes in v2:
time: 331 us; the launch traced here: 334 us
  starting transfers between devices  166 us (50%)
  Pallas kernels  163 us (49%)
  local copies, waits for them, and re-layouts  3.8 us (1%)
    ppermute x12, starting transfers between devices, passed_along(): lax.ppermute(value, axis, [(source, source + steps) for source in range(f...  166 us
    pallas_call x2, Pallas kernels, pair_terms(): pl.pallas_call(functools.partial(pair_kernel, REACH * here if inner else...  146 us
    pallas_call x1, Pallas kernels, own_terms(): pl.pallas_call(own_kernel, out_shape=[jax.ShapeDtypeStruct((1, 6, here, C...  17.2 us
  transfers between devices with their start and end apart: 12, of which 0 were waited for; matrix products, arithmetic and copies ran while one was open for 0% of the time, Pallas kernels for 44%

profile of v2, /device:TPU:127, one launch (start us, length us, event | category | flops | bytes accessed | tf_op | source)
XLA Modules:
  0.0 334.4 jit_solution(9831300018417864894)
XLA Ops:
  0.6 1.2 copy.13
  1.8 1.3 collective-permute-start
  3.1 1.3 collective-permute-start.1
  4.4 1.3 collective-permute-start.2
  5.7 3.2 collective-permute-start.3
  8.9 4.3 %collective-permute-start.4 = (f32[7,16,512]{2,1,0:T(8,128)S(1)}, f32[7,16,512]{2,1,0:T(8,128)S(1)}, u32[]{:S(2)}, u32[]{:S(2)}) collective-permute-start(f32[7,16,512]{2,1,0:T(8,128)S(1)} %bitcast.60), channel_id=1, source_target_pairs={{2,0},{3,1},{4,2},{5,3},{6,4},{7,5},{8,6},{9,7},{10,8},{11,9},{12,... | collective-permute-start | bytes 688136 | tf_op jit(solution)/shard_map/ppermute | solution.py:26
  13.3 0.8 copy.5.pairs
  14.7 0.0 collective-permute-done
  14.8 5.5 %collective-permute-start.5 = (f32[7,16,512]{2,1,0:T(8,128)S(1)}, f32[7,16,512]{2,1,0:T(8,128)S(1)}, u32[]{:S(2)}, u32[]{:S(2)}) collective-permute-start(f32[7,16,512]{2,1,0:T(8,128)S(1)} %bitcast.61), channel_id=1, source_target_pairs={{3,0},{4,1},{5,2},{6,3},{7,4},{8,5},{9,6},{10,7},{11,8},{12,9},{13... | collective-permute-start | bytes 688136 | tf_op jit(solution)/shard_map/ppermute | solution.py:26
  20.4 0.1 constant_dynamic-update-slice_fusion
  20.6 17.2 %own_terms.1 = (f32[1,6,16,512]{3,2,1,0:T(8,128)S(1)}, s32[192,2]{1,0:T(8,128)S(1)}, s32[2]{0:T(128)S(1)}) custom-call(s32[192,2]{1,0:T(8,128)S(1)} %copy.5.pairs, s32[1]{0:T(128)S(6)} %copy.20.count, s32[1]{0:T(128)} %bitcast.start, f32[1,7,16,512]{3,2,1,0:T(8,128)S(1)} %get-tuple-element.9.window), custom_call_target="tpu_custom_call" | custom-call | flops 12000000000 | bytes 1000000 | tf_op jit(solution)/shard_map/own_terms/pallas_call | solution.py:317
  37.8 0.0 collective-permute-done.3
  37.9 14.6 %outer_pairs.1 = f32[7,6,16,512]{3,2,1,0:T(8,128)S(1)} custom-call(s32[192,2]{1,0:T(8,128)S(1)} %get-tuple-element.6.order, s32[2]{0:T(128)S(1)} %get-tuple-element.7.bounds, f32[7,7,16,512]{3,2,1,0:T(8,128)S(1)} %bitcast_dynamic-update-slice_fusion.window), custom_call_target="tpu_custom_call" | custom-call | flops 149999992832 | bytes 1000000 | tf_op jit(solution)/shard_map/outer_pairs/pallas_call | solution.py:340
  52.5 0.1 slice_bitcast_fusion.5
  52.7 1.3 collective-permute-start.10
  54.0 1.3 collective-permute-start.11
  55.3 137.6 %collective-permute-start.6 = (f32[6,16,512]{2,1,0:T(8,128)S(1)}, f32[6,16,512]{2,1,0:T(8,128)S(1)}, u32[]{:S(2)}, u32[]{:S(2)}) collective-permute-start(f32[6,16,512]{2,1,0:T(8,128)S(1)} %get-tuple-element.10), channel_id=1, source_target_pairs={{3,0},{4,1},{5,2},{6,3},{7,4},{8,5},{9,6},{10,7},{11,8},{12,9},{13... | collective-permute-start | bytes 589832 | tf_op jit(solution)/shard_map/ppermute | solution.py:26
  192.8 1.3 collective-permute-start.7
  194.1 6.2 %collective-permute-start.8 = (f32[6,16,512]{2,1,0:T(8,128)S(1)}, f32[6,16,512]{2,1,0:T(8,128)S(1)}, u32[]{:S(2)}, u32[]{:S(2)}) collective-permute-start(f32[6,16,512]{2,1,0:T(8,128)S(1)} %get-tuple-element.14), channel_id=1, source_target_pairs={{1,0},{2,1},{3,2},{4,3},{5,4},{6,5},{7,6},{8,7},{9,8},{10,9},{11,1... | collective-permute-start | bytes 589832 | tf_op jit(solution)/shard_map/ppermute | solution.py:26
  200.3 1.3 collective-permute-start.9
  201.6 131.0 %inner_pairs.1 = f32[1,6,16,512]{3,2,1,0:T(8,128)S(1)} custom-call(s32[192,2]{1,0:T(8,128)S(1)} %get-tuple-element.6.order, s32[2]{0:T(128)S(1)} %get-tuple-element.7.bounds, f32[1,7,16,512]{3,2,1,0:T(8,128)S(1)} %copy-done.1), custom_call_target="tpu_custom_call" | custom-call | flops 16000000000 | bytes 1000000 | tf_op jit(solution)/shard_map/inner_pairs/pallas_call | solution.py:340
  332.7 0.2 fusion.6
  332.9 0.7 copy.8
  333.6 0.7 copy.9
  (23 shorter events, 0.2 us)
Async XLA Ops:
  0.6 19.8 %copy-start.2 = (f32[7,8192]{1,0:T(8,128)S(1)}, f32[7,8192]{1,0:T(8,128)}, u32[]{:S(2)}) copy-start(f32[7,8192]{1,0:T(8,128)} %param.3) | copy-start | bytes 688132
  1.8 13.0 %collective-permute-start = (f32[7,16,512]{2,1,0:T(8,128)S(1)}, f32[7,16,512]{2,1,0:T(8,128)S(1)}, u32[]{:S(2)}, u32[]{:S(2)}) collective-permute-start(f32[7,16,512]{2,1,0:T(8,128)S(1)} %bitcast.56), channel_id=1, source_target_pairs={{0,3},{1,4},{2,5},{3,6},{4,7},{5,8},{6,9},{7,10},{8,11},{9,12},{10... | collective-permute-start | bytes 688136 | tf_op jit(solution)/shard_map/ppermute | solution.py:26
  3.1 17.2 %collective-permute-start.1 = (f32[7,16,512]{2,1,0:T(8,128)S(1)}, f32[7,16,512]{2,1,0:T(8,128)S(1)}, u32[]{:S(2)}, u32[]{:S(2)}) collective-permute-start(f32[7,16,512]{2,1,0:T(8,128)S(1)} %bitcast.57), channel_id=1, source_target_pairs={{0,2},{1,3},{2,4},{3,5},{4,6},{5,7},{6,8},{7,9},{8,10},{9,11},{10,... | collective-permute-start | bytes 688136 | tf_op jit(solution)/shard_map/ppermute | solution.py:26
  4.4 16.0 %collective-permute-start.2 = (f32[7,16,512]{2,1,0:T(8,128)S(1)}, f32[7,16,512]{2,1,0:T(8,128)S(1)}, u32[]{:S(2)}, u32[]{:S(2)}) collective-permute-start(f32[7,16,512]{2,1,0:T(8,128)S(1)} %bitcast.58), channel_id=1, source_target_pairs={{0,1},{1,2},{2,3},{3,4},{4,5},{5,6},{6,7},{7,8},{8,9},{9,10},{10,1... | collective-permute-start | bytes 688136 | tf_op jit(solution)/shard_map/ppermute | solution.py:26
  5.7 32.1 %collective-permute-start.3 = (f32[7,16,512]{2,1,0:T(8,128)S(1)}, f32[7,16,512]{2,1,0:T(8,128)S(1)}, u32[]{:S(2)}, u32[]{:S(2)}) collective-permute-start(f32[7,16,512]{2,1,0:T(8,128)S(1)} %bitcast.59), channel_id=1, source_target_pairs={{1,0},{2,1},{3,2},{4,3},{5,4},{6,5},{7,6},{8,7},{9,8},{10,9},{11,1... | collective-permute-start | bytes 688136 | tf_op jit(solution)/shard_map/ppermute | solution.py:26
  8.9 28.9 %collective-permute-start.4 = (f32[7,16,512]{2,1,0:T(8,128)S(1)}, f32[7,16,512]{2,1,0:T(8,128)S(1)}, u32[]{:S(2)}, u32[]{:S(2)}) collective-permute-start(f32[7,16,512]{2,1,0:T(8,128)S(1)} %bitcast.60), channel_id=1, source_target_pairs={{2,0},{3,1},{4,2},{5,3},{6,4},{7,5},{8,6},{9,7},{10,8},{11,9},{12,... | collective-permute-start | bytes 688136 | tf_op jit(solution)/shard_map/ppermute | solution.py:26
  14.8 23.1 %collective-permute-start.5 = (f32[7,16,512]{2,1,0:T(8,128)S(1)}, f32[7,16,512]{2,1,0:T(8,128)S(1)}, u32[]{:S(2)}, u32[]{:S(2)}) collective-permute-start(f32[7,16,512]{2,1,0:T(8,128)S(1)} %bitcast.61), channel_id=1, source_target_pairs={{3,0},{4,1},{5,2},{6,3},{7,4},{8,5},{9,6},{10,7},{11,8},{12,9},{13... | collective-permute-start | bytes 688136 | tf_op jit(solution)/shard_map/ppermute | solution.py:26
  20.6 17.2 %copy-start = (f32[1,7,16,512]{3,2,1,0:T(8,128)}, f32[1,7,16,512]{3,2,1,0:T(8,128)S(1)}, u32[]{:S(2)}) copy-start(f32[1,7,16,512]{3,2,1,0:T(8,128)S(1)} %get-tuple-element.9.window) | copy-start | bytes 688132
  52.5 149.1 %copy-start.1 = (f32[1,7,16,512]{3,2,1,0:T(8,128)S(1)}, f32[1,7,16,512]{3,2,1,0:T(8,128)}, u32[]{:S(2)}) copy-start(f32[1,7,16,512]{3,2,1,0:T(8,128)} %copy-done) | copy-start | bytes 688132
  52.7 147.6 %collective-permute-start.10 = (f32[6,16,512]{2,1,0:T(8,128)S(1)}, f32[6,16,512]{2,1,0:T(8,128)S(1)}, u32[]{:S(2)}, u32[]{:S(2)}) collective-permute-start(f32[6,16,512]{2,1,0:T(8,128)S(1)} %get-tuple-element.12), channel_id=1, source_target_pairs={{0,2},{1,3},{2,4},{3,5},{4,6},{5,7},{6,8},{7,9},{8,10},{9,11},{10,... | collective-permute-start | bytes 589832 | tf_op jit(solution)/shard_map/ppermute | solution.py:26
  54.0 278.7 %collective-permute-start.11 = (f32[6,16,512]{2,1,0:T(8,128)S(1)}, f32[6,16,512]{2,1,0:T(8,128)S(1)}, u32[]{:S(2)}, u32[]{:S(2)}) collective-permute-start(f32[6,16,512]{2,1,0:T(8,128)S(1)} %get-tuple-element.11), channel_id=1, source_target_pairs={{0,3},{1,4},{2,5},{3,6},{4,7},{5,8},{6,9},{7,10},{8,11},{9,12},{10... | collective-permute-start | bytes 589832 | tf_op jit(solution)/shard_map/ppermute | solution.py:26
  55.3 277.4 %collective-permute-start.6 = (f32[6,16,512]{2,1,0:T(8,128)S(1)}, f32[6,16,512]{2,1,0:T(8,128)S(1)}, u32[]{:S(2)}, u32[]{:S(2)}) collective-permute-start(f32[6,16,512]{2,1,0:T(8,128)S(1)} %get-tuple-element.10), channel_id=1, source_target_pairs={{3,0},{4,1},{5,2},{6,3},{7,4},{8,5},{9,6},{10,7},{11,8},{12,9},{13... | collective-permute-start | bytes 589832 | tf_op jit(solution)/shard_map/ppermute | solution.py:26
  192.8 139.8 %collective-permute-start.7 = (f32[6,16,512]{2,1,0:T(8,128)S(1)}, f32[6,16,512]{2,1,0:T(8,128)S(1)}, u32[]{:S(2)}, u32[]{:S(2)}) collective-permute-start(f32[6,16,512]{2,1,0:T(8,128)S(1)} %get-tuple-element.15), channel_id=1, source_target_pairs={{2,0},{3,1},{4,2},{5,3},{6,4},{7,5},{8,6},{9,7},{10,8},{11,9},{12,... | collective-permute-start | bytes 589832 | tf_op jit(solution)/shard_map/ppermute | solution.py:26
  194.1 138.5 %collective-permute-start.8 = (f32[6,16,512]{2,1,0:T(8,128)S(1)}, f32[6,16,512]{2,1,0:T(8,128)S(1)}, u32[]{:S(2)}, u32[]{:S(2)}) collective-permute-start(f32[6,16,512]{2,1,0:T(8,128)S(1)} %get-tuple-element.14), channel_id=1, source_target_pairs={{1,0},{2,1},{3,2},{4,3},{5,4},{6,5},{7,6},{8,7},{9,8},{10,9},{11,1... | collective-permute-start | bytes 589832 | tf_op jit(solution)/shard_map/ppermute | solution.py:26
  200.3 132.4 %collective-permute-start.9 = (f32[6,16,512]{2,1,0:T(8,128)S(1)}, f32[6,16,512]{2,1,0:T(8,128)S(1)}, u32[]{:S(2)}, u32[]{:S(2)}) collective-permute-start(f32[6,16,512]{2,1,0:T(8,128)S(1)} %get-tuple-element.13), channel_id=1, source_target_pairs={{0,1},{1,2},{2,3},{3,4},{4,5},{5,6},{6,7},{7,8},{8,9},{9,10},{10,1... | collective-permute-start | bytes 589832 | tf_op jit(solution)/shard_map/ppermute | solution.py:26

commit v3 on v2

--- a/solution.py
+++ b/solution.py
@@ -12,7 +12,8 @@
 BATCH = 8
 ROWS = 8
 SUMS = 27
-STRIP = 128
+STRIP = 256
+LATE = 24
 PADDED = 32
 LANES = CLUSTER // 128
 inv_four_pi = 0.07957747154594767
@@ -104,7 +105,7 @@
     step = STRIP
     second = wide(table, aligned(source, ROWS))
     middle = centres[aligned(target, ROWS), :]
-    left = features(wide(table, aligned(target, ROWS)), middle, True).T.astype(bf16)
+    left = features(wide(table, aligned(target, ROWS)), middle, True).astype(bf16).T
     right = features(second, middle, False).astype(bf16)
     for row in range(0, CLUSTER, step):
         rho = jnp.maximum(matmul(left[row : row + step], right), second[3:4, :])
@@ -205,6 +206,7 @@
         second = jnp.clip(pairs[slot, 1] - anchor, 0, last)
         inner = jnp.logical_and(first >= REACH * here, second < (REACH + 1) * here)
         inner = jnp.logical_and(inner, jnp.logical_and(second >= REACH * here, first < (REACH + 1) * here))
+        inner = jnp.logical_and(inner, slot - front < LATE)
         where = jnp.where(inner, live - 1 - (slot - front), front)
         order[where, 0] = first
         order[where, 1] = second

time: 331 us -> 221 us (0.67)
  the two profiles are of different devices: /device:TPU:127 before, /device:TPU:6 now
where the time goes in v3:
time: 221 us; the launch traced here: 217 us
  Pallas kernels  155 us (70%)
  starting transfers between devices  57.1 us (26%)
  local copies, waits for them, and re-layouts  3.8 us (2%)
    pallas_call x2, Pallas kernels, pair_terms(): pl.pallas_call(functools.partial(pair_kernel, REACH * here if inner else...  137 us
    ppermute x12, starting transfers between devices, passed_along(): lax.ppermute(value, axis, [(source, source + steps) for source in range(f...  57.1 us
    pallas_call x1, Pallas kernels, own_terms(): pl.pallas_call(own_kernel, out_shape=[jax.ShapeDtypeStruct((1, 6, here, C...  17.3 us
  transfers between devices with their start and end apart: 12, of which 0 were waited for; matrix products, arithmetic and copies ran while one was open for 0% of the time, Pallas kernels for 19%

profile of v3, /device:TPU:6, one launch (start us, length us, event | category | flops | bytes accessed | tf_op | source)
XLA Modules:
  0.0 217.3 jit_solution(13465872219174259871)
XLA Ops:
  0.6 1.2 copy.13
  1.8 2.9 %collective-permute-start = (f32[7,16,512]{2,1,0:T(8,128)S(1)}, f32[7,16,512]{2,1,0:T(8,128)S(1)}, u32[]{:S(2)}, u32[]{:S(2)}) collective-permute-start(f32[7,16,512]{2,1,0:T(8,128)S(1)} %bitcast.56), channel_id=1, source_target_pairs={{0,3},{1,4},{2,5},{3,6},{4,7},{5,8},{6,9},{7,10},{8,11},{9,12},{10... | collective-permute-start | bytes 688136 | tf_op jit(solution)/shard_map/ppermute | solution.py:27
  4.7 3.5 %collective-permute-start.1 = (f32[7,16,512]{2,1,0:T(8,128)S(1)}, f32[7,16,512]{2,1,0:T(8,128)S(1)}, u32[]{:S(2)}, u32[]{:S(2)}) collective-permute-start(f32[7,16,512]{2,1,0:T(8,128)S(1)} %bitcast.57), channel_id=1, source_target_pairs={{0,2},{1,3},{2,4},{3,5},{4,6},{5,7},{6,8},{7,9},{8,10},{9,11},{10,... | collective-permute-start | bytes 688136 | tf_op jit(solution)/shard_map/ppermute | solution.py:27
  8.2 3.0 %collective-permute-start.2 = (f32[7,16,512]{2,1,0:T(8,128)S(1)}, f32[7,16,512]{2,1,0:T(8,128)S(1)}, u32[]{:S(2)}, u32[]{:S(2)}) collective-permute-start(f32[7,16,512]{2,1,0:T(8,128)S(1)} %bitcast.58), channel_id=1, source_target_pairs={{0,1},{1,2},{2,3},{3,4},{4,5},{5,6},{6,7},{7,8},{8,9},{9,10},{10,1... | collective-permute-start | bytes 688136 | tf_op jit(solution)/shard_map/ppermute | solution.py:27
  11.2 7.1 %collective-permute-start.3 = (f32[7,16,512]{2,1,0:T(8,128)S(1)}, f32[7,16,512]{2,1,0:T(8,128)S(1)}, u32[]{:S(2)}, u32[]{:S(2)}) collective-permute-start(f32[7,16,512]{2,1,0:T(8,128)S(1)} %bitcast.59), channel_id=1, source_target_pairs={{1,0},{2,1},{3,2},{4,3},{5,4},{6,5},{7,6},{8,7},{9,8},{10,9},{11,1... | collective-permute-start | bytes 688136 | tf_op jit(solution)/shard_map/ppermute | solution.py:27
  18.3 2.3 %collective-permute-start.4 = (f32[7,16,512]{2,1,0:T(8,128)S(1)}, f32[7,16,512]{2,1,0:T(8,128)S(1)}, u32[]{:S(2)}, u32[]{:S(2)}) collective-permute-start(f32[7,16,512]{2,1,0:T(8,128)S(1)} %bitcast.60), channel_id=1, source_target_pairs={{2,0},{3,1},{4,2},{5,3},{6,4},{7,5},{8,6},{9,7},{10,8},{11,9},{12,... | collective-permute-start | bytes 688136 | tf_op jit(solution)/shard_map/ppermute | solution.py:27
  20.7 0.8 copy.5.pairs
  22.1 2.3 %collective-permute-start.5 = (f32[7,16,512]{2,1,0:T(8,128)S(1)}, f32[7,16,512]{2,1,0:T(8,128)S(1)}, u32[]{:S(2)}, u32[]{:S(2)}) collective-permute-start(f32[7,16,512]{2,1,0:T(8,128)S(1)} %bitcast.61), channel_id=1, source_target_pairs={{3,0},{4,1},{5,2},{6,3},{7,4},{8,5},{9,6},{10,7},{11,8},{12,9},{13... | collective-permute-start | bytes 688136 | tf_op jit(solution)/shard_map/ppermute | solution.py:27
  24.5 0.0 collective-permute-done.1
  24.5 0.0 collective-permute-done.2
  24.6 0.1 constant_dynamic-update-slice_fusion
  24.7 17.3 %own_terms.1 = (f32[1,6,16,512]{3,2,1,0:T(8,128)S(1)}, s32[192,2]{1,0:T(8,128)S(1)}, s32[2]{0:T(128)S(1)}) custom-call(s32[192,2]{1,0:T(8,128)S(1)} %copy.5.pairs, s32[1]{0:T(128)S(6)} %copy.20.count, s32[1]{0:T(128)} %bitcast.start, f32[1,7,16,512]{3,2,1,0:T(8,128)S(1)} %get-tuple-element.9.window), custom_call_target="tpu_custom_call" | custom-call | flops 12000000000 | bytes 1000000 | tf_op jit(solution)/shard_map/own_terms/pallas_call | solution.py:319
  42.2 112.9 %outer_pairs.1 = f32[7,6,16,512]{3,2,1,0:T(8,128)S(1)} custom-call(s32[192,2]{1,0:T(8,128)S(1)} %get-tuple-element.6.order, s32[2]{0:T(128)S(1)} %get-tuple-element.7.bounds, f32[7,7,16,512]{3,2,1,0:T(8,128)S(1)} %bitcast_dynamic-update-slice_fusion.window), custom_call_target="tpu_custom_call" | custom-call | flops 149999992832 | bytes 1000000 | tf_op jit(solution)/shard_map/outer_pairs/pallas_call | solution.py:342
  155.1 0.1 slice_bitcast_fusion.5
  155.2 5.4 %collective-permute-start.10 = (f32[6,16,512]{2,1,0:T(8,128)S(1)}, f32[6,16,512]{2,1,0:T(8,128)S(1)}, u32[]{:S(2)}, u32[]{:S(2)}) collective-permute-start(f32[6,16,512]{2,1,0:T(8,128)S(1)} %get-tuple-element.12), channel_id=1, source_target_pairs={{0,2},{1,3},{2,4},{3,5},{4,6},{5,7},{6,8},{7,9},{8,10},{9,11},{10,... | collective-permute-start | bytes 589832 | tf_op jit(solution)/shard_map/ppermute | solution.py:27
  160.6 11.4 %collective-permute-start.11 = (f32[6,16,512]{2,1,0:T(8,128)S(1)}, f32[6,16,512]{2,1,0:T(8,128)S(1)}, u32[]{:S(2)}, u32[]{:S(2)}) collective-permute-start(f32[6,16,512]{2,1,0:T(8,128)S(1)} %get-tuple-element.11), channel_id=1, source_target_pairs={{0,3},{1,4},{2,5},{3,6},{4,7},{5,8},{6,9},{7,10},{8,11},{9,12},{10... | collective-permute-start | bytes 589832 | tf_op jit(solution)/shard_map/ppermute | solution.py:27
  172.0 1.9 collective-permute-start.6
  174.0 11.8 %collective-permute-start.7 = (f32[6,16,512]{2,1,0:T(8,128)S(1)}, f32[6,16,512]{2,1,0:T(8,128)S(1)}, u32[]{:S(2)}, u32[]{:S(2)}) collective-permute-start(f32[6,16,512]{2,1,0:T(8,128)S(1)} %get-tuple-element.15), channel_id=1, source_target_pairs={{2,0},{3,1},{4,2},{5,3},{6,4},{7,5},{8,6},{9,7},{10,8},{11,9},{12,... | collective-permute-start | bytes 589832 | tf_op jit(solution)/shard_map/ppermute | solution.py:27
  185.8 3.4 %collective-permute-start.8 = (f32[6,16,512]{2,1,0:T(8,128)S(1)}, f32[6,16,512]{2,1,0:T(8,128)S(1)}, u32[]{:S(2)}, u32[]{:S(2)}) collective-permute-start(f32[6,16,512]{2,1,0:T(8,128)S(1)} %get-tuple-element.14), channel_id=1, source_target_pairs={{1,0},{2,1},{3,2},{4,3},{5,4},{6,5},{7,6},{8,7},{9,8},{10,9},{11,1... | collective-permute-start | bytes 589832 | tf_op jit(solution)/shard_map/ppermute | solution.py:27
  189.1 2.0 collective-permute-start.9
  191.2 24.4 %inner_pairs.1 = f32[1,6,16,512]{3,2,1,0:T(8,128)S(1)} custom-call(s32[192,2]{1,0:T(8,128)S(1)} %get-tuple-element.6.order, s32[2]{0:T(128)S(1)} %get-tuple-element.7.bounds, f32[1,7,16,512]{3,2,1,0:T(8,128)S(1)} %copy-done.1), custom_call_target="tpu_custom_call" | custom-call | flops 16000000000 | bytes 1000000 | tf_op jit(solution)/shard_map/inner_pairs/pallas_call | solution.py:342
  215.7 0.2 fusion.6
  215.9 0.7 copy.8
  216.6 0.7 copy.9
  (23 shorter events, 0.2 us)
Async XLA Ops:
  0.6 24.0 %copy-start.2 = (f32[7,8192]{1,0:T(8,128)S(1)}, f32[7,8192]{1,0:T(8,128)}, u32[]{:S(2)}) copy-start(f32[7,8192]{1,0:T(8,128)} %param.3) | copy-start | bytes 688132
  1.8 20.3 %collective-permute-start = (f32[7,16,512]{2,1,0:T(8,128)S(1)}, f32[7,16,512]{2,1,0:T(8,128)S(1)}, u32[]{:S(2)}, u32[]{:S(2)}) collective-permute-start(f32[7,16,512]{2,1,0:T(8,128)S(1)} %bitcast.56), channel_id=1, source_target_pairs={{0,3},{1,4},{2,5},{3,6},{4,7},{5,8},{6,9},{7,10},{8,11},{9,12},{10... | collective-permute-start | bytes 688136 | tf_op jit(solution)/shard_map/ppermute | solution.py:27
  4.7 19.8 %collective-permute-start.1 = (f32[7,16,512]{2,1,0:T(8,128)S(1)}, f32[7,16,512]{2,1,0:T(8,128)S(1)}, u32[]{:S(2)}, u32[]{:S(2)}) collective-permute-start(f32[7,16,512]{2,1,0:T(8,128)S(1)} %bitcast.57), channel_id=1, source_target_pairs={{0,2},{1,3},{2,4},{3,5},{4,6},{5,7},{6,8},{7,9},{8,10},{9,11},{10,... | collective-permute-start | bytes 688136 | tf_op jit(solution)/shard_map/ppermute | solution.py:27
  8.2 16.3 %collective-permute-start.2 = (f32[7,16,512]{2,1,0:T(8,128)S(1)}, f32[7,16,512]{2,1,0:T(8,128)S(1)}, u32[]{:S(2)}, u32[]{:S(2)}) collective-permute-start(f32[7,16,512]{2,1,0:T(8,128)S(1)} %bitcast.58), channel_id=1, source_target_pairs={{0,1},{1,2},{2,3},{3,4},{4,5},{5,6},{6,7},{7,8},{8,9},{9,10},{10,1... | collective-permute-start | bytes 688136 | tf_op jit(solution)/shard_map/ppermute | solution.py:27
  11.2 30.8 %collective-permute-start.3 = (f32[7,16,512]{2,1,0:T(8,128)S(1)}, f32[7,16,512]{2,1,0:T(8,128)S(1)}, u32[]{:S(2)}, u32[]{:S(2)}) collective-permute-start(f32[7,16,512]{2,1,0:T(8,128)S(1)} %bitcast.59), channel_id=1, source_target_pairs={{1,0},{2,1},{3,2},{4,3},{5,4},{6,5},{7,6},{8,7},{9,8},{10,9},{11,1... | collective-permute-start | bytes 688136 | tf_op jit(solution)/shard_map/ppermute | solution.py:27
  18.3 23.7 %collective-permute-start.4 = (f32[7,16,512]{2,1,0:T(8,128)S(1)}, f32[7,16,512]{2,1,0:T(8,128)S(1)}, u32[]{:S(2)}, u32[]{:S(2)}) collective-permute-start(f32[7,16,512]{2,1,0:T(8,128)S(1)} %bitcast.60), channel_id=1, source_target_pairs={{2,0},{3,1},{4,2},{5,3},{6,4},{7,5},{8,6},{9,7},{10,8},{11,9},{12,... | collective-permute-start | bytes 688136 | tf_op jit(solution)/shard_map/ppermute | solution.py:27
  22.1 20.0 %collective-permute-start.5 = (f32[7,16,512]{2,1,0:T(8,128)S(1)}, f32[7,16,512]{2,1,0:T(8,128)S(1)}, u32[]{:S(2)}, u32[]{:S(2)}) collective-permute-start(f32[7,16,512]{2,1,0:T(8,128)S(1)} %bitcast.61), channel_id=1, source_target_pairs={{3,0},{4,1},{5,2},{6,3},{7,4},{8,5},{9,6},{10,7},{11,8},{12,9},{13... | collective-permute-start | bytes 688136 | tf_op jit(solution)/shard_map/ppermute | solution.py:27
  24.7 17.3 %copy-start = (f32[1,7,16,512]{3,2,1,0:T(8,128)}, f32[1,7,16,512]{3,2,1,0:T(8,128)S(1)}, u32[]{:S(2)}) copy-start(f32[1,7,16,512]{3,2,1,0:T(8,128)S(1)} %get-tuple-element.9.window) | copy-start | bytes 688132
  155.1 36.1 %copy-start.1 = (f32[1,7,16,512]{3,2,1,0:T(8,128)S(1)}, f32[1,7,16,512]{3,2,1,0:T(8,128)}, u32[]{:S(2)}) copy-start(f32[1,7,16,512]{3,2,1,0:T(8,128)} %copy-done) | copy-start | bytes 688132
  155.2 33.9 %collective-permute-start.10 = (f32[6,16,512]{2,1,0:T(8,128)S(1)}, f32[6,16,512]{2,1,0:T(8,128)S(1)}, u32[]{:S(2)}, u32[]{:S(2)}) collective-permute-start(f32[6,16,512]{2,1,0:T(8,128)S(1)} %get-tuple-element.12), channel_id=1, source_target_pairs={{0,2},{1,3},{2,4},{3,5},{4,6},{5,7},{6,8},{7,9},{8,10},{9,11},{10,... | collective-permute-start | bytes 589832 | tf_op jit(solution)/shard_map/ppermute | solution.py:27
  160.6 55.0 %collective-permute-start.11 = (f32[6,16,512]{2,1,0:T(8,128)S(1)}, f32[6,16,512]{2,1,0:T(8,128)S(1)}, u32[]{:S(2)}, u32[]{:S(2)}) collective-permute-start(f32[6,16,512]{2,1,0:T(8,128)S(1)} %get-tuple-element.11), channel_id=1, source_target_pairs={{0,3},{1,4},{2,5},{3,6},{4,7},{5,8},{6,9},{7,10},{8,11},{9,12},{10... | collective-permute-start | bytes 589832 | tf_op jit(solution)/shard_map/ppermute | solution.py:27
  172.0 43.6 %collective-permute-start.6 = (f32[6,16,512]{2,1,0:T(8,128)S(1)}, f32[6,16,512]{2,1,0:T(8,128)S(1)}, u32[]{:S(2)}, u32[]{:S(2)}) collective-permute-start(f32[6,16,512]{2,1,0:T(8,128)S(1)} %get-tuple-element.10), channel_id=1, source_target_pairs={{3,0},{4,1},{5,2},{6,3},{7,4},{8,5},{9,6},{10,7},{11,8},{12,9},{13... | collective-permute-start | bytes 589832 | tf_op jit(solution)/shard_map/ppermute | solution.py:27
  174.0 41.7 %collective-permute-start.7 = (f32[6,16,512]{2,1,0:T(8,128)S(1)}, f32[6,16,512]{2,1,0:T(8,128)S(1)}, u32[]{:S(2)}, u32[]{:S(2)}) collective-permute-start(f32[6,16,512]{2,1,0:T(8,128)S(1)} %get-tuple-element.15), channel_id=1, source_target_pairs={{2,0},{3,1},{4,2},{5,3},{6,4},{7,5},{8,6},{9,7},{10,8},{11,9},{12,... | collective-permute-start | bytes 589832 | tf_op jit(solution)/shard_map/ppermute | solution.py:27
  185.8 29.9 %collective-permute-start.8 = (f32[6,16,512]{2,1,0:T(8,128)S(1)}, f32[6,16,512]{2,1,0:T(8,128)S(1)}, u32[]{:S(2)}, u32[]{:S(2)}) collective-permute-start(f32[6,16,512]{2,1,0:T(8,128)S(1)} %get-tuple-element.14), channel_id=1, source_target_pairs={{1,0},{2,1},{3,2},{4,3},{5,4},{6,5},{7,6},{8,7},{9,8},{10,9},{11,1... | collective-permute-start | bytes 589832 | tf_op jit(solution)/shard_map/ppermute | solution.py:27
  189.1 26.5 %collective-permute-start.9 = (f32[6,16,512]{2,1,0:T(8,128)S(1)}, f32[6,16,512]{2,1,0:T(8,128)S(1)}, u32[]{:S(2)}, u32[]{:S(2)}) collective-permute-start(f32[6,16,512]{2,1,0:T(8,128)S(1)} %get-tuple-element.13), channel_id=1, source_target_pairs={{0,1},{1,2},{2,3},{3,4},{4,5},{5,6},{6,7},{7,8},{8,9},{9,10},{10,1... | collective-permute-start | bytes 589832 | tf_op jit(solution)/shard_map/ppermute | solution.py:27
